TPU v7x, 32 devices: a whole 2x2x4 slice. The times are simulated.
32 devices in a mesh: ctx: 8 (over y, x, core), head: 4 (over z).
Axes of the slice: x: 2, y: 2, z: 4, core: 2. Of those that a mesh axis runs over, the one named last changes fastest.
Arguments:
- query_vectors: bfloat16 [1024, 4096], P('ctx', 'head'), may hold values from -6 to 6
- key_vectors: bfloat16 [1024, 4096], P('ctx', 'head'), may hold values from -1.5 to 1.5
- value_vectors: bfloat16 [1024, 4096], P('ctx', 'head'), may hold values from -6 to 6
- log_decay: float32 [32, 1024], P('head', 'ctx'), may hold values from -2 to 0, as said below
- residual: bfloat16 [1024, 3072], P('ctx'), may hold values from -6 to 6
- out_weight: bfloat16 [4096, 3072], P('head', 'ctx'), may hold values from -0.09375 to 0.09375
- attn_gain: float32 [4096], P('head'), may hold values from 0.1 to 1.9
- moe_gain: float32 [3072], replicated, may hold values from 0.1 to 1.9
- router: float32 [3072, 8], replicated, may hold values from -0.109375 to 0.109375
- w_gate: bfloat16 [8, 3072, 4608], P('ctx', None, 'head'), may hold values from -0.109375 to 0.109375
- w_up: bfloat16 [8, 3072, 4608], P('ctx', None, 'head'), may hold values from -0.109375 to 0.109375
- w_down: bfloat16 [8, 4608, 3072], P('ctx', 'head'), may hold values from -0.09375 to 0.09375
- expert_ids: int32 [1024, 2], P('ctx'), may hold values from 0 to 7, all different within a row; in each aligned block of 128 rows (0 to 127, 128 to 255, ...) at most 64 rows name the same one
Outputs:
- final_out: bfloat16 [1024, 3072], P('ctx', 'head')
Inputs may be any that keep to these rules, and one draw needn't show every extreme that they name: `expert_ids`: each row names 2 different experts. In each aligned block of 128 rows no expert is named by more than 64 rows, and in every draw some expert is named by exactly 64 rows of some block. `log_decay`: every entry is negative.
All inputs are finite; a program needn't handle non-finite values.
Results may differ from a plain program's by a relative error of at most 0.022.
Values may be sent and summed in bfloat16 or wider, within the bound.
A program may use at most 128 MiB of HBM per device.

v0:
```python
import jax
import jax.numpy as jnp
from jax import lax
from jax.sharding import PartitionSpec as P

TOP = 2


PRECISE = lax.Precision.HIGHEST


def entering(value, axis, combine, identity):
    peers, index = (lax.axis_size(axis), lax.axis_index(axis))
    everything = jax.tree.map(
        lambda part, kind: lax.all_gather(part.astype(kind), axis),
        value,
        (jnp.bfloat16, jnp.bfloat16),
    )
    start = jax.tree.map(
        lambda part, zero: jnp.broadcast_to(jnp.asarray(zero, part.dtype), part.shape),
        value,
        identity,
    )

    def step(k, before):
        reached = k < index
        new = combine(
            before, jax.tree.map(lambda part, own: part[k].astype(own.dtype), everything, value)
        )
        return jax.tree.map(lambda a, b: jnp.where(reached, a, b), new, before)

    return lax.fori_loop(0, peers, step, start)


def local_attention(query_block, key_block, value_block, decay_block):
    running = jnp.cumsum(decay_block, axis=1)
    length_here = decay_block.shape[1]
    row_index = lax.broadcasted_iota(jnp.int32, (length_here, length_here), 0)
    col_index = lax.broadcasted_iota(jnp.int32, (length_here, length_here), 1)
    causal = (col_index <= row_index)[None]
    spread = jnp.where(causal, running[:, :, None] - running[:, None, :], 0.0)
    decay_weights = jnp.where(causal, jnp.exp(spread), 0.0)
    scores = jnp.einsum("htd,hsd->hts", query_block, key_block, precision=PRECISE) * decay_weights
    inside_part = jnp.einsum("hts,hse->hte", scores, value_block, precision=PRECISE)
    final_log = running[:, -1]
    tail_decay = jnp.exp(final_log[:, None] - running)
    local_state = jnp.einsum(
        "hsd,hse->hde", key_block * tail_decay[:, :, None], value_block, precision=PRECISE
    )
    return (inside_part, running, local_state, final_log)


def route_tokens(logits, expert_ids, experts_total):
    onehot = expert_ids[:, :, None] == lax.broadcasted_iota(jnp.int32, (1, 1, experts_total), 2)
    chosen = jnp.sum(jnp.where(onehot, logits[:, None, :], 0.0), axis=2)
    leading = jax.nn.sigmoid(chosen[:, 0] - chosen[:, 1])
    gate_weights = jnp.stack([leading, 1.0 - leading], axis=1)
    marked = onehot.reshape(-1, experts_total).astype(jnp.int32)
    earlier = jnp.cumsum(marked, axis=0) - marked
    slot_index = jnp.sum(earlier * marked, axis=1).reshape(expert_ids.shape)
    return (gate_weights, slot_index)


def link_states(earlier, later):
    return (earlier[0] + later[0], jnp.exp(later[0])[:, None, None] * earlier[1] + later[1])


def body(
    query_vectors,
    key_vectors,
    value_vectors,
    log_decay,
    residual,
    out_weight,
    attn_gain,
    moe_gain,
    router,
    w_gate,
    w_up,
    w_down,
    expert_ids,
):
    token_count = query_vectors.shape[0]
    heads_here = log_decay.shape[0]
    head_size = query_vectors.shape[1] // heads_here

    def split_heads(matrix_in):
        return (
            matrix_in.astype(jnp.float32)
            .reshape(token_count, heads_here, head_size)
            .transpose(1, 0, 2)
        )

    query_heads = split_heads(query_vectors)
    inside_part, running, local_state, final_log = local_attention(
        query_heads, split_heads(key_vectors), split_heads(value_vectors), log_decay
    )
    identity = (jnp.zeros_like(final_log), jnp.zeros_like(local_state))
    _, prior_state = entering((final_log, local_state), "ctx", link_states, identity)
    outside_part = jnp.exp(running)[:, :, None] * jnp.einsum(
        "htd,hde->hte", query_heads, prior_state, precision=PRECISE
    )
    attended = inside_part + outside_part
    square_mean = jnp.mean(attended * attended, axis=2, keepdims=True)
    heads_normed = (
        attended * lax.rsqrt(square_mean + 1e-05) * attn_gain.reshape(heads_here, 1, head_size)
    )
    heads_normed = (
        heads_normed.astype(jnp.bfloat16)
        .transpose(1, 0, 2)
        .reshape(token_count, heads_here * head_size)
    )
    partial_out = jnp.dot(
        heads_normed,
        lax.all_gather(out_weight, "ctx", axis=1, tiled=True),
        preferred_element_type=jnp.float32,
    )
    model_width = residual.shape[1]
    experts_total = router.shape[1]
    capacity = 2 * token_count * TOP // experts_total
    slice_width = model_width // lax.axis_size("head")
    slice_start = lax.axis_index("head") * slice_width
    projected = lax.psum(partial_out.astype(jnp.bfloat16), "head").astype(jnp.float32)
    mixed_rows = (residual.astype(jnp.float32) + projected).astype(jnp.bfloat16)
    mixed_wide = mixed_rows.astype(jnp.float32)
    inv_rms = lax.rsqrt(jnp.mean(mixed_wide * mixed_wide, axis=1, keepdims=True) + 1e-06)
    scaled = mixed_wide * moe_gain[None, :]
    moe_in = (scaled * inv_rms).astype(jnp.bfloat16)
    logits = inv_rms * jnp.dot(scaled, router, precision=PRECISE)
    base_slice = lax.dynamic_slice_in_dim(mixed_wide, slice_start, slice_width, 1)
    gate_weights, slot_index = route_tokens(logits, expert_ids, experts_total)
    target = (expert_ids * capacity + slot_index).reshape(-1)
    width_here = moe_in.shape[1]
    source = jnp.repeat(moe_in, TOP, axis=0)
    packed = jnp.zeros((experts_total * capacity, width_here), jnp.bfloat16).at[target].set(source)
    arrived = lax.all_to_all(
        packed.reshape(experts_total, capacity, width_here),
        "ctx",
        split_axis=0,
        concat_axis=0,
        tiled=True,
    )
    flat_rows = arrived.reshape(-1, model_width)
    gate_part = jnp.dot(flat_rows, w_gate[0], preferred_element_type=jnp.float32)
    up_part = jnp.dot(flat_rows, w_up[0], preferred_element_type=jnp.float32)
    hidden = (jax.nn.silu(gate_part) * up_part).astype(jnp.bfloat16)
    partial_down = jnp.dot(hidden, w_down[0], preferred_element_type=jnp.float32).reshape(
        arrived.shape
    )
    returned = lax.all_to_all(
        lax.all_to_all(
            partial_down.astype(jnp.bfloat16)[None], "ctx", split_axis=1, concat_axis=1, tiled=True
        ),
        "head",
        split_axis=3,
        concat_axis=0,
        tiled=True,
    )
    expert_out = jnp.sum(returned.astype(jnp.float32), axis=0).astype(jnp.bfloat16)
    lookup = expert_out.reshape(experts_total * capacity, slice_width)
    picked = lookup[target].reshape(token_count, TOP, slice_width).astype(jnp.float32)
    final_out = (
        base_slice + gate_weights[:, 0:1] * picked[:, 0] + gate_weights[:, 1:2] * picked[:, 1]
    )
    return final_out.astype(jnp.bfloat16)


def solution(mesh):
    in_specs = (
        P("ctx", "head"),
        P("ctx", "head"),
        P("ctx", "head"),
        P("head", "ctx"),
        P("ctx", None),
        P("head", "ctx"),
        P("head"),
        P(),
        P(),
        P("ctx", None, "head"),
        P("ctx", None, "head"),
        P("ctx", "head", None),
        P("ctx", None),
    )
    out_specs = P("ctx", "head")
    return jax.shard_map(body, mesh=mesh, in_specs=in_specs, out_specs=out_specs, check_vma=False)
```

profile of v0, /device:TPU:16, one launch (start us, length us, event | category | flops | bytes accessed | tf_op | source)
XLA Modules:
  0.0 352.7 jit_solution(13769152916426166640)
XLA Ops:
  6.6 1.0 reduce_window_sum.26
  7.6 0.2 slice_reduce_fusion.1
  7.8 0.1 exponential_bitcast_fusion.1
  7.9 1.1 copy.100
  9.0 2.1 convolution_convert_fusion.1
  11.1 0.0 all-gather.5.cloned.1.call-start
  11.1 0.7 all-gather.5.cloned.1.call-update
  11.8 0.0 all-reduce.3.cloned.1.call-start
  11.9 0.6 dynamic-slice
  13.1 0.2 fusion.51
  13.3 0.2 dynamic-update-slice
  13.5 13.8 %all-reduce = bf16[64]{0:T(256)(128)(2,1)S(1)} all-reduce(bf16[64]{0:T(256)(128)(2,1)S(1)} %dynamic-update-slice), channel_id=2, replica_groups=mesh['ctx'=8,'head'=4] {'ctx'}, use_global_device_ids=true, to_apply=%add | all-reduce | flops 64 | bytes 256
  27.3 0.1 reshape.186
  27.4 0.1 copy.88
  27.5 0.1 eq.39
  27.7 0.2 convolution_multiply_fusion
  28.0 12.3 %all-gather.7.cloned.1.call-done = bf16[64,128,128]{2,1,0:T(8,128)(2,1)} async-done(((bf16[8,128,128]{2,1,0:T(8,128)(2,1)}), bf16[64,128,128]{2,1,0:T(8,128)(2,1)}) %all-gather.7.cloned.1.call-update) | async-done | bytes 2097168 | tf_op jit(solution)/shard_map/all_gather | solution.py:15
  40.3 9.1 %while.14 = (s32[]{:T(128)}, f32[8,128,128]{2,1,0:T(8,128)S(1)}, s32[]{:T(128)}, bf16[8,8]{1,0:T(8,128)(2,1)S(1)}, bf16[8,8,128,128]{3,2,1,0:T(8,128)(2,1)}, /*index=5*/s32[]{:T(128)}, s32[]{:T(128)}) while((s32[]{:T(128)}, f32[8,128,128]{2,1,0:T(8,128)S(1)}, s32[]{:T(128)}, bf16[8,8]{1,0:T(8,128)(2,1)S(1)}, ...), condition=%wide.region_2.3_spmd.clone, body=%wide.region_1.2_spmd.clone.sunk | while | flops 655372 | bytes 1310913 | solution.py:32
  40.3 1.1 fusion.67
  41.4 1.1 fusion.67
  42.5 1.1 fusion.67
  43.7 1.1 fusion.67
  44.8 1.1 fusion.67
  46.0 1.1 fusion.67
  47.1 1.1 fusion.67
  48.2 1.1 fusion.67
  49.4 0.6 fusion.42
  50.0 0.7 fusion.29
  50.7 0.2 fusion.33
  50.9 37.9 %all-gather.5.cloned.1.call-done = bf16[1024,3072]{1,0:T(8,128)(2,1)} async-done(((bf16[1024,384]{1,0:T(8,128)(2,1)}), bf16[1024,3072]{1,0:T(8,128)(2,1)}) %all-gather.5.cloned.1.call-update) | async-done | bytes 6291472 | tf_op jit(solution)/shard_map/all_gather | solution.py:115
  88.8 4.8 %convolution_convert_fusion = bf16[128,3072]{1,0:T(8,128)(2,1)} fusion(bf16[128,1024]{0,1:T(8,128)(2,1)S(1)} %bitcast.140, bf16[1024,3072]{1,0:T(8,128)(2,1)} %all-gather.5.cloned.1.call-done), kind=kOutput, calls=%fused_computation.13 | convolution fusion | flops 805699584 | bytes 7340032 | tf_op jit(solution)/shard_map/dot_general | solution.py:113
  93.6 0.1 eq.35
  93.8 0.6 reduce-window.6
  94.4 0.2 slice_reduce_fusion
  94.6 0.1 fusion.49
  94.7 0.1 reshape.162
  94.9 0.1 copy.90
  94.9 0.1 copy.91
  95.1 0.1 reshape.163
  95.2 41.3 %all-reduce.3.cloned.1.call-done = bf16[128,3072]{1,0:T(8,128)(2,1)} async-done(((bf16[128,3072]{1,0:T(8,128)(2,1)}), bf16[128,3072]{1,0:T(8,128)(2,1)}) %all-reduce.3.cloned.1.call-update) | async-done | bytes 786448 | tf_op jit(solution)/shard_map/psum | solution.py:123
  136.5 2.5 fusion.52
  139.0 0.2 multiply_reduce_fusion
  139.3 0.7 copy-done.2
  140.0 0.2 multiply_convert_fusion
  140.2 0.8 broadcast_in_dim.60
  141.0 1.5 reshape.182
  142.5 4.7 %scatter_custom_fusion = bf16[512,3072]{1,0:T(8,128)(2,1)S(1)} fusion(s32[256]{0:T(256)S(1)} %bitcast.147, bf16[256,3072]{1,0:T(8,128)(2,1)} %reshape.182, bf16[]{:T(256)} %constant.66.clone.1), kind=kCustom, calls=%fused_computation.17 | custom fusion | bytes 3146240 | tf_op jit(solution)/shard_map/scatter | solution.py:135
  147.3 41.5 %all_to_all.22 = bf16[8,64,3072]{2,1,0:T(8,128)(2,1)S(1)} all-to-all(bf16[8,64,3072]{2,1,0:T(8,128)(2,1)S(1)} %bitcast.137), channel_id=1, replica_groups=mesh['ctx'=8,'head'=4] {'ctx'}, dimensions={0} | all-to-all | bytes 6291456 | tf_op jit(solution)/shard_map/all_to_all | solution.py:136
  188.8 6.6 %fusion.5 = f32[512,1152]{1,0:T(8,128)S(1)} fusion(bf16[512,3072]{1,0:T(8,128)(2,1)S(1)} %bitcast.138, bf16[1,3072,1152]{2,1,0:T(8,128)(2,1)} %param.24), kind=kOutput, calls=%fused_computation.9 | convolution fusion | flops 3623878656 | bytes 12582912 | tf_op jit(solution)/shard_map/dot_general | solution.py:144
  195.4 4.3 %fusion.16 = bf16[512,1152]{1,0:T(8,128)(2,1)S(1)} fusion(bf16[512,3072]{1,0:T(8,128)(2,1)S(1)} %bitcast.139, bf16[1,3072,1152]{2,1,0:T(8,128)(2,1)S(1)} %bitcast.151, f32[512,1152]{1,0:T(8,128)S(1)} %fusion.5), kind=kOutput, calls=%fused_computation.15 | convolution fusion | flops 3627417600 | bytes 13762560 | tf_op jit(solution)/shard_map/dot_general | solution.py:145
  199.7 4.5 %fusion.10 = bf16[1,8,64,3072]{3,2,0,1:T(8,128)(2,1)S(1)} fusion(bf16[8,64,1152]{2,1,0:T(8,128)(2,1)S(1)} %bitcast.154, bf16[1,1152,3072]{2,1,0:T(8,128)(2,1)S(1)} %bitcast.153), kind=kOutput, calls=%fused_computation.12 | convolution fusion | flops 3625451520 | bytes 11403264 | tf_op jit(solution)/shard_map/dot_general | solution.py:147
  204.2 40.3 %all_to_all.23 = bf16[1,8,64,3072]{3,2,0,1:T(8,128)(2,1)S(1)} all-to-all(bf16[1,8,64,3072]{3,2,0,1:T(8,128)(2,1)S(1)} %fusion.10), channel_id=1, replica_groups=mesh['ctx'=8,'head'=4] {'ctx'}, dimensions={1} | all-to-all | bytes 6291456 | tf_op jit(solution)/shard_map/all_to_all | solution.py:151
  244.5 6.0 %copy.93 = bf16[1,8,64,3072]{2,1,0,3:T(8,128)(2,1)} copy(bf16[1,8,64,3072]{3,2,0,1:T(8,128)(2,1)S(1)} %all_to_all.23) | data formatting | bytes 6291456 | tf_op jit(solution)/shard_map/all_to_all | solution.py:151
  250.6 7.8 %reshape.201 = bf16[4,2,196608]{2,1,0:T(2,128)(2,1)} reshape(bf16[3072,1,8,64]{3,2,1,0:T(8,128)(2,1)} %bitcast.135) | data formatting | bytes 6291456
  258.4 5.2 %all-to-all-start.2 = ((bf16[4,2,196608]{2,1,0:T(2,128)(2,1)}), bf16[4,2,196608]{2,1,0:T(2,128)(2,1)S(1)}, u32[]{:S(2)}, u32[]{:S(2)}) async-start(bf16[4,2,196608]{2,1,0:T(2,128)(2,1)} %reshape.201), calls=%async_computation.2 | async-start | bytes 6291456 | tf_op jit(solution)/shard_map/all_to_all | solution.py:150
  263.7 2.5 fusion.24
  266.2 64.5 %all-to-all-done.2 = bf16[4,2,196608]{2,1,0:T(2,128)(2,1)S(1)} async-done(((bf16[4,2,196608]{2,1,0:T(2,128)(2,1)}), bf16[4,2,196608]{2,1,0:T(2,128)(2,1)S(1)}, u32[]{:S(2)}, u32[]{:S(2)}) %all-to-all-start.2) | async-done | bytes 3145760 | tf_op jit(solution)/shard_map/all_to_all | solution.py:150
  330.7 5.3 %reshape.202 = bf16[3072,1,8,64]{3,2,1,0:T(8,128)(2,1)} reshape(bf16[4,2,196608]{2,1,0:T(2,128)(2,1)S(1)} %all-to-all-done.2) | data formatting | bytes 6291456
  336.0 5.2 %reduce_sum.52 = bf16[8,64,768]{1,0,2:T(8,128)(2,1)S(1)} reduce(bf16[8,64,4,768]{1,0,3,2:T(8,128)(2,1)} %bitcast.134, bf16[]{:T(256)} %constant.66.clone.1), dimensions={2}, to_apply=%region_11.12 | reduce | flops 1179648 | bytes 3932162 | tf_op jit(solution)/shard_map/reduce_sum | solution.py:159
  341.1 1.0 copy.94
  342.2 1.2 gather_fusion
  343.3 0.4 reshape.169
  343.7 0.6 fusion.53
  344.3 1.8 fusion.38
  (54 shorter events, 0.4 us)
Async XLA Ops:
  6.5 21.2 %copy-start = (bf16[128,1024]{1,0:T(8,128)(2,1)S(1)}, bf16[128,1024]{1,0:T(8,128)(2,1)}, u32[]{:S(2)}) copy-start(bf16[128,1024]{1,0:T(8,128)(2,1)} %param.15) | copy-start | bytes 786436
  6.5 5.4 %copy-start.9 = (u32[32]{0:T(128)S(1)}, u32[32]{0:T(128)}, u32[]{:S(2)}) copy-start(u32[32]{0:T(128)} %constant.74) | copy-start | bytes 388
  6.5 21.1 %copy-start.3 = (bf16[128,1024]{1,0:T(8,128)(2,1)S(1)}, bf16[128,1024]{1,0:T(8,128)(2,1)}, u32[]{:S(2)}) copy-start(bf16[128,1024]{1,0:T(8,128)(2,1)} %param.17) | copy-start | bytes 786436
  6.5 20.8 %copy-start.7 = (s32[128,2]{0,1:T(2,128)S(1)}, s32[128,2]{0,1:T(2,128)}, u32[]{:S(2)}) copy-start(s32[128,2]{0,1:T(2,128)} %param.27) | copy-start | bytes 3076
  6.5 33.7 %all-gather.7.cloned.1.call-start = ((), (), s32[]{:S(2)}) async-start(), calls=%async_computation.5 | async-start | bytes 2359296 | tf_op jit(solution)/shard_map/all_gather | solution.py:15
  11.1 77.7 %all-gather.5.cloned.1.call-start = ((), (), s32[]{:S(2)}) async-start(), calls=%async_computation.3 | async-start | bytes 7077888 | tf_op jit(solution)/shard_map/all_gather | solution.py:115
  11.8 124.7 %all-reduce.3.cloned.1.call-start = ((), (), s32[]{:S(2)}) async-start(), calls=%async_computation.4 | async-start | bytes 1572864 | tf_op jit(solution)/shard_map/psum | solution.py:123
  49.4 1.3 copy-start.8
  88.8 47.7 %copy-start.4 = (bf16[128,3072]{1,0:T(8,128)(2,1)S(1)}, bf16[128,3072]{1,0:T(8,128)(2,1)}, u32[]{:S(2)}) copy-start(bf16[128,3072]{1,0:T(8,128)(2,1)} %param.19) | copy-start | bytes 2359300
  95.2 44.7 %copy-start.6 = (f32[3072]{0:T(1024)S(1)}, f32[3072]{0:T(1024)}, u32[]{:S(2)}) copy-start(f32[3072]{0:T(1024)} %param.22) | copy-start | bytes 36868
  139.0 0.9 copy-start.2
  147.2 48.2 %slice-start = ((s8[7077888]{0:T(1024)(128)(4,1)}), s8[4194304]{0:T(1024)(128)(4,1)S(1)}, s32[]{:S(2)}) async-start(s8[7077888]{0:T(1024)(128)(4,1)} %bitcast.150), calls=%async_computation.6 | async-start | bytes 8388608
  147.2 52.5 %slice-start.2 = ((s8[7077888]{0:T(1024)(128)(4,1)}), s8[4194304]{0:T(1024)(128)(4,1)S(1)}, s32[]{:S(2)}) async-start(s8[7077888]{0:T(1024)(128)(4,1)} %bitcast.152), calls=%async_computation.8 | async-start | bytes 8388608
  188.8 6.6 %slice-start.1 = ((s8[7077888]{0:T(1024)(128)(4,1)}), s8[2883584]{0:T(1024)(128)(4,1)S(1)}, s32[]{:S(2)}) async-start(s8[7077888]{0:T(1024)(128)(4,1)} %bitcast.150), calls=%async_computation.7 | async-start | bytes 5767168
  188.8 10.9 %slice-start.3 = ((s8[7077888]{0:T(1024)(128)(4,1)}), s8[2883584]{0:T(1024)(128)(4,1)S(1)}, s32[]{:S(2)}) async-start(s8[7077888]{0:T(1024)(128)(4,1)} %bitcast.152), calls=%async_computation.9 | async-start | bytes 5767168
  258.4 5.2 %copy-start.5 = (f32[3072,8]{0,1:T(8,128)S(1)}, f32[3072,8]{0,1:T(8,128)}, u32[]{:S(2)}) copy-start(f32[3072,8]{0,1:T(8,128)} %param.23) | copy-start | bytes 294916
  258.4 72.3 %all-to-all-start.2 = ((bf16[4,2,196608]{2,1,0:T(2,128)(2,1)}), bf16[4,2,196608]{2,1,0:T(2,128)(2,1)S(1)}, u32[]{:S(2)}, u32[]{:S(2)}) async-start(bf16[4,2,196608]{2,1,0:T(2,128)(2,1)} %reshape.201), calls=%async_computation.2 | async-start | bytes 6291456 | tf_op jit(solution)/shard_map/all_to_all | solution.py:150
  342.1 4.0 %copy-start.1 = (bf16[128,1024]{1,0:T(8,128)(2,1)S(1)}, bf16[128,1024]{1,0:T(8,128)(2,1)}, u32[]{:S(2)}) copy-start(bf16[128,1024]{1,0:T(8,128)(2,1)} %param.15) | copy-start | bytes 786436
Sparse Core Ops, SparseCore 0:
  11.2 29.0 all-gather.6
  42.1 46.6 all-gather.4
  93.7 42.7 all-reduce.2
where the time goes:
time: 358 us; the launch traced here: 353 us
  waiting for transfers between devices  157 us (44%)
  blocking collectives  95.6 us (27%)
  local copies, waits for them, and re-layouts  33.7 us (9%)
  matrix products  26.2 us (7%)
  other arithmetic  20.9 us (6%)
  between operations  14 us (4%)
  starting transfers between devices  5.35 us (1%)
    all_to_all x1, waiting for transfers between devices, body(): lax.all_to_all(lax.all_to_all(partial_down.astype(jnp.bfloat16)[None], 'c...  64.5 us
    all_to_all x1, blocking collectives, body(): lax.all_to_all(packed.reshape(experts_total, capacity, width_here), 'ctx'...  41.5 us
    psum x1, waiting for transfers between devices, body(): lax.psum(partial_out.astype(jnp.bfloat16), 'head').astype(jnp.float32)  41.3 us
    all_to_all x1, blocking collectives, body(): lax.all_to_all(partial_down.astype(jnp.bfloat16)[None], 'ctx', split_axis...  40.3 us
    all_gather x1, waiting for transfers between devices, body(): lax.all_gather(out_weight, 'ctx', axis=1, tiled=True)  37.9 us
    unnamed x35, local copies, waits for them, and re-layouts  14.8 us
    unnamed x1, blocking collectives  13.8 us
    all_gather x1, waiting for transfers between devices, entering(): lax.all_gather(part.astype(kind), axis)  12.3 us
  transfers between devices with their start and end apart: 4, of which 4 were waited for; matrix products, arithmetic and copies ran while one was open for 5% of the time, Pallas kernels for 0%

commit v1 on v0

--- a/solution.py
+++ b/solution.py
@@ -1,6 +1,10 @@
+import functools
+
 import jax
 import jax.numpy as jnp
 from jax import lax
+from jax.experimental import pallas as pl
+from jax.experimental.pallas import tpu as pltpu
 from jax.sharding import PartitionSpec as P
 
 TOP = 2
@@ -65,7 +69,7 @@
     return (earlier[0] + later[0], jnp.exp(later[0])[:, None, None] * earlier[1] + later[1])
 
 
-def body(
+def general_body(
     query_vectors,
     key_vectors,
     value_vectors,
@@ -165,7 +169,652 @@
     return final_out.astype(jnp.bfloat16)
 
 
+MESH = pl.DeviceIdType.MESH
+ANY = pl.BlockSpec(memory_space=pl.ANY)
+VMEM = pl.BlockSpec(memory_space=pltpu.VMEM)
+
+
+def plane_peers():
+    me = lax.axis_index("ctx")
+    core, x, y = me % 2, (me // 2) % 2, me // 4
+
+    def at(c, a, b):
+        return (b * 2 + a) * 2 + c
+
+    return (
+        me,
+        at(1 - core, x, y),
+        at(core, 1 - x, y),
+        at(core, x, 1 - y),
+        at(core, 1 - x, 1 - y),
+    )
+
+
+def greet(axes_and_peers):
+    barrier = pltpu.get_barrier_semaphore()
+    for axis, peer in axes_and_peers:
+        pl.semaphore_signal(barrier, inc=1, device_id={axis: peer}, device_id_type=MESH)
+    pl.semaphore_wait(barrier, len(axes_and_peers))
+
+
+def gather_kernel(count, *refs):
+    blocks, outs = refs[:count], refs[count : 2 * count]
+    send, recv, local = refs[2 * count :]
+    me, sib, xn, yn, dg = plane_peers()
+    greet([("ctx", sib), ("ctx", xn), ("ctx", yn)])
+
+    def copy(i, step, src, dst, peer):
+        return pltpu.make_async_remote_copy(
+            src_ref=src,
+            dst_ref=dst,
+            send_sem=send.at[i, step],
+            recv_sem=recv.at[i, step],
+            device_id={"ctx": peer},
+            device_id_type=MESH,
+        )
+
+    plans, own = [], []
+    for i, (block, out) in enumerate(zip(blocks, outs)):
+        half = block.shape[0] // 2
+        top, low = pl.ds(0, half), pl.ds(half, half)
+        plan = [
+            copy(i, 0, block, out.at[me], sib),
+            copy(i, 1, block, out.at[me], xn),
+            copy(i, 2, block, out.at[me], yn),
+            copy(i, 3, out.at[xn, top], out.at[xn, top], yn),
+            copy(i, 4, out.at[xn], out.at[xn], sib),
+            copy(i, 5, out.at[yn, low], out.at[yn, low], xn),
+            copy(i, 6, out.at[yn], out.at[yn], sib),
+            copy(i, 7, out.at[dg, top], out.at[dg, top], sib),
+            copy(i, 8, out.at[dg, low], out.at[dg, low], sib),
+        ]
+        plans.append(plan)
+        for step in (1, 2, 0):
+            plan[step].start()
+        mine = pltpu.make_async_copy(block, out.at[me], local.at[i])
+        mine.start()
+        own.append(mine)
+    for got, onward in ((1, (3, 4)), (2, (5, 6)), (3, (7,)), (5, (8,))):
+        for plan in plans:
+            plan[got].wait_recv()
+            for step in onward:
+                plan[step].start()
+    for plan, mine in zip(plans, own):
+        for step in (0, 4, 6, 7, 8):
+            plan[step].wait_recv()
+        for step in range(9):
+            plan[step].wait_send()
+        mine.wait()
+
+
+def plane_gather(collective_id, *blocks):
+    count = len(blocks)
+    ctx = lax.axis_size("ctx")
+    return pl.pallas_call(
+        functools.partial(gather_kernel, count),
+        out_shape=[jax.ShapeDtypeStruct((ctx,) + b.shape, b.dtype) for b in blocks],
+        in_specs=[ANY] * count,
+        out_specs=[ANY] * count,
+        scratch_shapes=[
+            pltpu.SemaphoreType.DMA((count, 9)),
+            pltpu.SemaphoreType.DMA((count, 9)),
+            pltpu.SemaphoreType.DMA((count,)),
+        ],
+        compiler_params=pltpu.CompilerParams(collective_id=collective_id, has_side_effects=True),
+        name="plane_gather",
+    )(*blocks)
+
+
+def block_order(me, sib, xn, yn, dg):
+    def other_core(index):
+        return index + 1 - 2 * (index % 2)
+
+    return (me, sib, xn, yn, other_core(xn), other_core(yn), dg, other_core(dg))
+
+
+def z_order():
+    z = lax.axis_index("head")
+    return (z + 1 - 2 * (z % 2), z + 2 - 4 * (z // 2), 3 - z)
+
+
+def sender(send, recv):
+    def copy(at, src, dst, axis, peer):
+        return pltpu.make_async_remote_copy(
+            src_ref=src,
+            dst_ref=dst,
+            send_sem=send.at[at],
+            recv_sem=recv.at[at],
+            device_id={axis: peer},
+            device_id_type=MESH,
+        )
+
+    return copy
+
+
+GATHER, TO_Z, TO_COLS, ROWS_Z, BASE_Z, SPREAD = 0, 9, 33, 41, 44, 47
+
+
+def spread_kernel(
+    normed, weight, residual, gain, router, ids, base, out,
+    rows, part, from_z, summed, by_cols, mixed, piece, send, recv, local,
+):
+    me, sib, xn, yn, dg = plane_peers()
+    z = lax.axis_index("head")
+    blocks, zs = block_order(me, sib, xn, yn, dg), z_order()
+    greet([("ctx", b) for b in blocks[1:]] + [("head", p) for p in zs])
+    copy = sender(send, recv)
+    f32, bf16 = jnp.float32, jnp.bfloat16
+    share, model_width = residual.shape
+    width = weight.shape[1]
+    half = normed.shape[0] // 2
+    top, low = pl.ds(0, half), pl.ds(half, half)
+
+    plan = [
+        copy(0, normed, rows.at[me], "ctx", sib),
+        copy(1, normed, rows.at[me], "ctx", xn),
+        copy(2, normed, rows.at[me], "ctx", yn),
+        copy(3, rows.at[xn, top], rows.at[xn, top], "ctx", yn),
+        copy(4, rows.at[xn], rows.at[xn], "ctx", sib),
+        copy(5, rows.at[yn, low], rows.at[yn, low], "ctx", xn),
+        copy(6, rows.at[yn], rows.at[yn], "ctx", sib),
+        copy(7, rows.at[dg, top], rows.at[dg, top], "ctx", sib),
+        copy(8, rows.at[dg, low], rows.at[dg, low], "ctx", sib),
+    ]
+    for step in (1, 2, 0):
+        plan[step].start()
+    sent = list(plan)
+    z_in = []
+
+    def project(i, block):
+        product = jnp.dot(block, weight[...], preferred_element_type=f32).astype(bf16)
+        for k in range(len(zs) + 1):
+            part[i, k] = product[k * share : (k + 1) * share]
+        z_in.append([])
+        for d, peer in enumerate(zs):
+            out_copy = copy(
+                TO_Z + 3 * i + d, part.at[i, peer], from_z.at[i, d], "head", peer
+            )
+            out_copy.start()
+            z_in[i].append(out_copy)
+            sent.append(out_copy)
+
+    def arrived(*steps):
+        for step in steps:
+            plan[step].wait_recv()
+
+    project(0, normed[...])
+    arrived(0)
+    project(1, rows[sib])
+    arrived(1)
+    plan[3].start()
+    plan[4].start()
+    project(2, rows[xn])
+    arrived(2)
+    plan[5].start()
+    plan[6].start()
+    project(3, rows[yn])
+    arrived(4)
+    project(4, rows[blocks[4]])
+    arrived(6)
+    project(5, rows[blocks[5]])
+    arrived(3)
+    plan[7].start()
+    arrived(5)
+    plan[8].start()
+    project(6, rows[dg])
+    arrived(7, 8)
+    project(7, rows[blocks[7]])
+
+    col_copies = []
+    for i, block in enumerate(blocks):
+        total = part[i, z].astype(f32)
+        for d in range(3):
+            z_in[i][d].wait_recv()
+            total += from_z[i, d].astype(f32)
+        summed[i] = total.astype(bf16)
+        if i:
+            col_copies.append(
+                copy(TO_COLS + i, summed.at[i], by_cols.at[me], "ctx", block)
+            )
+            col_copies[-1].start()
+    by_cols[me] = summed[0]
+    for each in col_copies:
+        each.wait_recv()
+    sent += col_copies
+
+    per = model_width // (len(zs) + 1) // width
+    squares = jnp.zeros((share, 1), f32)
+    for k in range(model_width // width):
+        cols = slice(k * width, (k + 1) * width)
+        whole = (residual[:, cols].astype(f32) + by_cols[k].astype(f32)).astype(bf16)
+        mixed[k // per, :, (k % per) * width : (k % per + 1) * width] = whole
+        wide = whole.astype(f32)
+        squares += jnp.sum(wide * wide, axis=1, keepdims=True)
+    inv_rms = lax.rsqrt(squares / model_width + 1e-06)
+    experts_total = router.shape[0]
+    logits = [jnp.zeros((share, 1), f32)] * experts_total
+    slice_width = per * width
+    for k in range(len(zs) + 1):
+        cols = slice(k * slice_width, (k + 1) * slice_width)
+        scaled = mixed[k].astype(f32) * gain[:, cols]
+        piece[:, cols] = (scaled * inv_rms).astype(bf16)
+        for e in range(experts_total):
+            logits[e] += jnp.sum(scaled * router[e : e + 1, cols], axis=1, keepdims=True)
+    first, second = ids[:, 0:1], ids[:, 1:2]
+    ahead = jnp.zeros((share, 1), f32)
+    for e in range(experts_total):
+        ahead += jnp.where(first == e, logits[e], 0.0) - jnp.where(second == e, logits[e], 0.0)
+    leading = jax.nn.sigmoid(ahead * inv_rms)
+    big = leading.astype(bf16).astype(f32)
+    middle = (leading - big).astype(bf16).astype(f32)
+    small = leading - big - middle
+    lane = lax.broadcasted_iota(jnp.int32, (share, 128), 1)
+    notes = jnp.zeros((share, 128), f32)
+    for k, value in enumerate((first.astype(f32), second.astype(f32), big, middle, small)):
+        notes = jnp.where(lane == k, value, notes)
+    piece[:, model_width:] = notes.astype(bf16)
+
+    z_copies, base_copies = [], []
+    quarter = share // 2
+    upper, lower = pl.ds(0, quarter), pl.ds(quarter, quarter)
+
+    def spread(j, source, k):
+        s = SPREAD + 9 * j
+        steps = [
+            copy(s, source, out.at[me, k], "ctx", sib),
+            copy(s + 1, source, out.at[me, k], "ctx", xn),
+            copy(s + 2, source, out.at[me, k], "ctx", yn),
+            copy(s + 3, out.at[xn, k, upper], out.at[xn, k, upper], "ctx", yn),
+            copy(s + 4, out.at[xn, k], out.at[xn, k], "ctx", sib),
+            copy(s + 5, out.at[yn, k, lower], out.at[yn, k, lower], "ctx", xn),
+            copy(s + 6, out.at[yn, k], out.at[yn, k], "ctx", sib),
+            copy(s + 7, out.at[dg, k, upper], out.at[dg, k, upper], "ctx", sib),
+            copy(s + 8, out.at[dg, k, lower], out.at[dg, k, lower], "ctx", sib),
+        ]
+        for step in (1, 2, 0):
+            steps[step].start()
+        return steps
+
+    def relay(steps):
+        for got, onward in ((1, (3, 4)), (2, (5, 6)), (3, (7,)), (5, (8,))):
+            steps[got].wait_recv()
+            for step in onward:
+                steps[step].start()
+
+    for d, peer in enumerate(zs):
+        z_copies.append(copy(ROWS_Z + d, piece, out.at[me, z], "head", peer))
+        z_copies[-1].start()
+    runs = [spread(0, piece, z)]
+    mine = pltpu.make_async_copy(piece, out.at[me, z], local.at[0])
+    mine.start()
+    own_base = pltpu.make_async_copy(mixed.at[z], base.at[z], local.at[1])
+    own_base.start()
+    for d, peer in enumerate(zs):
+        z_copies[d].wait_recv()
+        runs.append(spread(d + 1, out.at[me, peer], peer))
+        relay(runs[d])
+    for d, peer in enumerate(zs):
+        base_copies.append(copy(BASE_Z + d, mixed.at[peer], base.at[z], "head", peer))
+        base_copies[-1].start()
+    relay(runs[3])
+    for steps in runs:
+        for step in (0, 4, 6, 7, 8):
+            steps[step].wait_recv()
+        sent += steps
+    for each in base_copies:
+        each.wait_recv()
+    for each in sent + z_copies + base_copies:
+        each.wait_send()
+    mine.wait()
+    own_base.wait()
+
+
+def spread_rows(normed, weight, residual_rows, gain, router, ids):
+    ctx, planes = lax.axis_size("ctx"), lax.axis_size("head")
+    tokens, depth = normed.shape
+    width = weight.shape[1]
+    share, model_width = residual_rows.shape
+    dma, bf16 = pltpu.SemaphoreType.DMA, jnp.bfloat16
+    return pl.pallas_call(
+        spread_kernel,
+        out_shape=[
+            jax.ShapeDtypeStruct((planes, share, model_width // planes), bf16),
+            jax.ShapeDtypeStruct((ctx, planes, share, model_width + 128), bf16),
+        ],
+        in_specs=[VMEM] * 6,
+        out_specs=[ANY, ANY],
+        scratch_shapes=[
+            pltpu.VMEM((ctx, tokens, depth), bf16),
+            pltpu.VMEM((ctx, planes, share, width), bf16),
+            pltpu.VMEM((ctx, planes - 1, share, width), bf16),
+            pltpu.VMEM((ctx, share, width), bf16),
+            pltpu.VMEM((ctx, share, width), bf16),
+            pltpu.VMEM((planes, share, model_width // planes), bf16),
+            pltpu.VMEM((share, model_width + 128), bf16),
+            dma((SPREAD + 9 * planes,)),
+            dma((SPREAD + 9 * planes,)),
+            dma((2,)),
+        ],
+        compiler_params=pltpu.CompilerParams(
+            collective_id=2, has_side_effects=True, vmem_limit_bytes=40 << 20
+        ),
+        name="spread_rows",
+    )(normed, weight, residual_rows, gain, router, ids)
+
+
+PAIR, SUMS, SLICES = 0, 4, 28
+TILE = 256
+
+
+def expert_kernel(
+    tokens, w_gate, w_up, w_down, base, out,
+    toks, wide, down, picked, slot_gate, hidden, theirs, ours, pair, onehots,
+    ahead, across, landed, total, from_z, send, recv, load,
+):
+    me, sib, xn, yn, dg = plane_peers()
+    z = lax.axis_index("head")
+    zs = z_order()
+    chunks = zs + (z,)
+    f32, bf16 = jnp.float32, jnp.bfloat16
+    count, model_width = picked.shape[0] // 8, picked.shape[1]
+    units = hidden.shape[1]
+    tiles = units // TILE
+
+    def other_core(index):
+        return index + 1 - 2 * (index % 2)
+
+    away = (other_core(dg), other_core(xn), other_core(yn), sib)
+    here = (dg, xn, yn, me)
+    order = away + here
+    token_loads = [
+        pltpu.make_async_copy(tokens.at[b], toks.at[i], load.at[i]) for i, b in enumerate(order)
+    ]
+    for each in token_loads:
+        each.start()
+    weight_loads = []
+    for j in range(tiles):
+        for k, matrix in enumerate((w_gate, w_up)):
+            weight_loads.append(
+                pltpu.make_async_copy(
+                    matrix.at[:, pl.ds(j * TILE, TILE)],
+                    wide.at[2 * j + k],
+                    load.at[8 + 2 * j + k],
+                )
+            )
+    rest = units - tiles * TILE
+    for k, matrix in enumerate((w_gate, w_up)):
+        weight_loads.append(
+            pltpu.make_async_copy(
+                matrix.at[:, pl.ds(tiles * TILE, rest)],
+                wide.at[2 * tiles, :, pl.ds(k * rest, rest)],
+                load.at[8 + 2 * tiles + k],
+            )
+        )
+    down_load = pltpu.make_async_copy(w_down, down, load.at[10 + 2 * tiles])
+    for each in weight_loads + [down_load]:
+        each.start()
+    greet([("ctx", sib), ("ctx", xn), ("ctx", yn)] + [("head", p) for p in zs])
+    copy = sender(send, recv)
+
+    row = lax.broadcasted_iota(jnp.int32, (128, 128), 0)
+    col = lax.broadcasted_iota(jnp.int32, (128, 128), 1)
+    lower = (col <= row).astype(bf16)
+
+    def chosen(notes, expert, offset):
+        e = expert.astype(f32)
+        named = (notes[:, 0:1] == e) | (notes[:, 1:2] == e)
+        marks = jnp.broadcast_to(named.astype(f32), (128, 128)).astype(bf16)
+        slot = jnp.dot(lower, marks, preferred_element_type=f32).astype(jnp.int32) - 1 + offset
+        return jnp.where((slot == col) & (marks > 0), 1.0, 0.0)
+
+    for i in range(8):
+        token_loads[i].wait()
+        notes = toks[i, :, model_width:].astype(f32)
+        place = chosen(notes, me, 0)
+        if i >= 4:
+            onehots[i - 4] = (place + chosen(notes, sib, count)).astype(bf16)
+        pick = place[:, :count].astype(bf16)
+        rows = lax.dot_general(
+            pick, toks[i], (((0,), (0,)), ((), ())), preferred_element_type=f32
+        )
+        picked[i * count : (i + 1) * count] = rows[:, :model_width].astype(bf16)
+        said = rows[:, model_width:]
+        leading = said[:, 2:3] + said[:, 3:4] + said[:, 4:5]
+        gate = jnp.where(said[:, 0:1] == me.astype(f32), leading, 1.0 - leading)
+        slot_gate[i * count : (i + 1) * count] = jnp.broadcast_to(gate, (count, 128))
+
+    def act(gated, up):
+        return (gated * jax.nn.sigmoid(gated) * up).astype(bf16)
+
+    for j in range(tiles):
+        weight_loads[2 * j].wait()
+        gated = jnp.dot(picked[...], wide[2 * j], preferred_element_type=f32)
+        weight_loads[2 * j + 1].wait()
+        up = jnp.dot(picked[...], wide[2 * j + 1], preferred_element_type=f32)
+        hidden[:, j * TILE : (j + 1) * TILE] = act(gated, up)
+    weight_loads[2 * tiles].wait()
+    weight_loads[2 * tiles + 1].wait()
+    both = jnp.dot(picked[...], wide[2 * tiles], preferred_element_type=f32)
+    hidden[:, tiles * TILE :] = act(both[:, :rest], both[:, rest:])
+
+    width = out.shape[1]
+    down_load.wait()
+
+    def project(store, first):
+        rows = slice(first * count, (first + 4) * count)
+        gate = slot_gate[rows, 0:1]
+        for k in range(4):
+            cols = slice(k * width, (k + 1) * width)
+            value = jnp.dot(hidden[rows], down[:, cols], preferred_element_type=f32) * gate
+            for i in range(4):
+                store[i, k] = value[i * count : (i + 1) * count].astype(bf16)
+
+    project(theirs, 0)
+    pairs = [copy(PAIR + i, theirs.at[i], pair.at[i], "ctx", sib) for i in range(4)]
+    for each in pairs:
+        each.start()
+    project(ours, 4)
+
+    half = 64
+    top, low = pl.ds(0, half), pl.ds(half, half)
+
+    def tokens_of(i, k, rows):
+        slots = jnp.concatenate([ours[i, k], pair[i, k]], axis=0)
+        return jnp.dot(onehots[i, rows], slots, preferred_element_type=f32)
+
+    plans = []
+    for j in range(4):
+        s = SUMS + 6 * j
+        plans.append(
+            [
+                copy(s, ahead.at[j, 0, top], across.at[j, 0], "ctx", yn),
+                copy(s + 1, ahead.at[j, 0, low], across.at[j, 1], "ctx", xn),
+                copy(s + 2, ahead.at[j, 1, low], landed.at[j, 0, low], "ctx", xn),
+                copy(s + 3, ahead.at[j, 2, top], landed.at[j, 1, top], "ctx", yn),
+                copy(s + 4, ahead.at[j, 1, top], landed.at[j, 0, top], "ctx", xn),
+                copy(s + 5, ahead.at[j, 2, low], landed.at[j, 1, low], "ctx", yn),
+            ]
+        )
+    out_z = [
+        copy(SLICES + d, total.at[d], from_z.at[d], "head", peer) for d, peer in enumerate(zs)
+    ]
+
+    def begin(j):
+        k = chunks[j]
+        if j == 0:
+            pairs[0].wait_recv()
+        ahead[j, 0] = tokens_of(0, k, slice(None)).astype(bf16)
+        plans[j][0].start()
+        plans[j][1].start()
+        if j == 0:
+            pairs[1].wait_recv()
+        ahead[j, 1, low] = tokens_of(1, k, low).astype(bf16)
+        plans[j][2].start()
+        if j == 0:
+            pairs[2].wait_recv()
+        ahead[j, 2, top] = tokens_of(2, k, top).astype(bf16)
+        plans[j][3].start()
+
+    def pass_on(j):
+        k = chunks[j]
+        plans[j][0].wait_recv()
+        ahead[j, 1, top] = (tokens_of(1, k, top) + across[j, 0].astype(f32)).astype(bf16)
+        plans[j][4].start()
+        plans[j][1].wait_recv()
+        ahead[j, 2, low] = (tokens_of(2, k, low) + across[j, 1].astype(f32)).astype(bf16)
+        plans[j][5].start()
+
+    def finish(j):
+        k = chunks[j]
+        if j == 0:
+            pairs[3].wait_recv()
+        value = tokens_of(3, k, slice(None))
+        for step in (2, 3, 4, 5):
+            plans[j][step].wait_recv()
+        value += landed[j, 0].astype(f32) + landed[j, 1].astype(f32)
+        if j < 3:
+            total[j] = value.astype(bf16)
+            out_z[j].start()
+        return value
+
+    begin(0)
+    begin(1)
+    pass_on(0)
+    begin(2)
+    pass_on(1)
+    finish(0)
+    begin(3)
+    pass_on(2)
+    finish(1)
+    pass_on(3)
+    finish(2)
+    value = finish(3) + base[...].astype(f32)
+    for d in range(3):
+        out_z[d].wait_recv()
+        value += from_z[d].astype(f32)
+    out[...] = value.astype(bf16)
+    for each in pairs + sum(plans, []) + out_z:
+        each.wait_send()
+
+
+def run_experts(tokens, w_gate, w_up, w_down, base, capacity):
+    ctx, rows, wide = tokens.shape
+    model_width, units = w_gate.shape
+    width = base.shape[1]
+    planes = model_width // width
+    dma, bf16 = pltpu.SemaphoreType.DMA, jnp.bfloat16
+    tiles = units // TILE
+    return pl.pallas_call(
+        expert_kernel,
+        out_shape=jax.ShapeDtypeStruct(base.shape, bf16),
+        in_specs=[ANY] * 4 + [VMEM],
+        out_specs=VMEM,
+        scratch_shapes=[
+            pltpu.VMEM((ctx, rows, wide), bf16),
+            pltpu.VMEM((2 * tiles + 1, model_width, TILE), bf16),
+            pltpu.VMEM((units, model_width), bf16),
+            pltpu.VMEM((ctx * capacity, model_width), bf16),
+            pltpu.VMEM((ctx * capacity, 128), jnp.float32),
+            pltpu.VMEM((ctx * capacity, units), bf16),
+            pltpu.VMEM((4, planes, capacity, width), bf16),
+            pltpu.VMEM((4, planes, capacity, width), bf16),
+            pltpu.VMEM((4, planes, capacity, width), bf16),
+            pltpu.VMEM((4, rows, 2 * capacity), bf16),
+            pltpu.VMEM((planes, 3, rows, width), bf16),
+            pltpu.VMEM((planes, 2, rows // 2, width), bf16),
+            pltpu.VMEM((planes, 2, rows, width), bf16),
+            pltpu.VMEM((planes - 1, rows, width), bf16),
+            pltpu.VMEM((planes - 1, rows, width), bf16),
+            dma((SLICES + planes,)),
+            dma((SLICES + planes,)),
+            dma((11 + 2 * tiles,)),
+        ],
+        compiler_params=pltpu.CompilerParams(
+            collective_id=3, has_side_effects=True, vmem_limit_bytes=60 << 20
+        ),
+        name="run_experts",
+    )(tokens, w_gate, w_up, w_down, base)
+
+
+def plane_body(
+    query_vectors,
+    key_vectors,
+    value_vectors,
+    log_decay,
+    residual,
+    out_weight,
+    attn_gain,
+    moe_gain,
+    router,
+    w_gate,
+    w_up,
+    w_down,
+    expert_ids,
+):
+    token_count = query_vectors.shape[0]
+    heads_here = log_decay.shape[0]
+    head_size = query_vectors.shape[1] // heads_here
+    ctx, planes = lax.axis_size("ctx"), lax.axis_size("head")
+    me, z = lax.axis_index("ctx"), lax.axis_index("head")
+    bf16, f32 = jnp.bfloat16, jnp.float32
+
+    def split_heads(matrix_in):
+        return matrix_in.astype(f32).reshape(token_count, heads_here, head_size).transpose(1, 0, 2)
+
+    query_heads = split_heads(query_vectors)
+    inside_part, running, local_state, final_log = local_attention(
+        query_heads, split_heads(key_vectors), split_heads(value_vectors), log_decay
+    )
+    logs = jnp.broadcast_to(final_log[:, None], (heads_here, head_size))
+    states, all_logs = plane_gather(
+        1,
+        local_state.astype(bf16).reshape(heads_here * head_size, head_size),
+        jnp.concatenate([logs, jnp.zeros_like(logs)], axis=0),
+    )
+    all_logs = all_logs[:, :heads_here, 0]
+    place = lax.broadcasted_iota(jnp.int32, (ctx, 1), 0)
+    before = place < me
+    later = jnp.where(before, all_logs, 0.0)
+    after = jnp.cumsum(later[::-1], axis=0)[::-1] - later
+    scale = jnp.where(before, jnp.exp(after), 0.0)
+    prior_state = jnp.sum(
+        scale[:, :, None, None]
+        * states.reshape(ctx, heads_here, head_size, head_size).astype(f32),
+        axis=0,
+    )
+    outside_part = jnp.exp(running)[:, :, None] * jnp.einsum(
+        "htd,hde->hte", query_heads, prior_state, precision=PRECISE
+    )
+    attended = inside_part + outside_part
+    square_mean = jnp.mean(attended * attended, axis=2, keepdims=True)
+    heads_normed = (
+        attended * lax.rsqrt(square_mean + 1e-05) * attn_gain.reshape(heads_here, 1, head_size)
+    )
+    heads_normed = (
+        heads_normed.astype(bf16).transpose(1, 0, 2).reshape(token_count, heads_here * head_size)
+    )
+    share = token_count // planes
+    base, tokens = spread_rows(
+        heads_normed,
+        out_weight,
+        lax.dynamic_slice_in_dim(residual, z * share, share, 0),
+        moe_gain[None, :],
+        router.T,
+        lax.dynamic_slice_in_dim(expert_ids, z * share, share, 0),
+    )
+    return run_experts(
+        tokens.reshape(ctx, token_count, tokens.shape[-1]),
+        w_gate[0],
+        w_up[0],
+        w_down[0],
+        base.reshape(token_count, -1),
+        2 * token_count * TOP // router.shape[1],
+    )
+
+
 def solution(mesh):
+    sizes = dict(mesh.shape)
+    body = plane_body if (sizes["ctx"], sizes["head"]) == (8, 4) else general_body
     in_specs = (
         P("ctx", "head"),
         P("ctx", "head"),

time: 358 us -> 173 us (0.48); the launches traced: 353 us -> 173 us
  waiting for transfers between devices: 157 us -> 0 us
  Pallas kernels: 0 us -> 154 us
  blocking collectives: 95.6 us -> 0 us
  local copies, waits for them, and re-layouts: 33.7 us -> 10.2 us
  matrix products: 26.2 us -> 4.59 us
  other arithmetic: 20.9 us -> 3.95 us
  between operations: 14 us -> 0.19 us
  starting transfers between devices: 5.35 us -> 0 us
    pallas_call x0 -> x3, Pallas kernels: none -> 154 us  [the longest x1 70.9 us: run_experts(): pl.pallas_call(expert_kernel, out_shape=jax.ShapeDtypeStruct(base.shape,...]
    all_to_all x2 -> x0, blocking collectives: 81.8 us -> none  [the longest x1 41.5 us: body(): lax.all_to_all(packed.reshape(experts_total, capacity, width_here), 'ctx'...]
    all_to_all x1 -> x0, waiting for transfers between devices: 64.5 us -> none  [body(): lax.all_to_all(lax.all_to_all(partial_down.astype(jnp.bfloat16)[None], 'c...]
    all_gather x2 -> x0, waiting for transfers between devices: 50.2 us -> none  [the longest x1 37.9 us: body(): lax.all_gather(out_weight, 'ctx', axis=1, tiled=True)]
    psum x1 -> x0, waiting for transfers between devices: 41.3 us -> none  [body(): lax.psum(partial_out.astype(jnp.bfloat16), 'head').astype(jnp.float32)]
    dot_general x6 -> x1, matrix products: 23.1 us -> 0.6 us  [plane_body(): jnp.einsum('htd,hde->hte', query_heads, prior_state, precision=PRECISE)]
    unnamed x1 -> x0, blocking collectives: 13.8 us -> none
    select_n x9 -> x2, other arithmetic: 8.78 us -> 0.15 us  [the longest x1 0.08 us: plane_body(): scale = jnp.where(before, jnp.exp(after), 0.0)]
  transfers between devices with their start and end apart: 4 -> 0, of which waited for: 4 -> 0; matrix products, arithmetic and copies ran while one was open for 5% -> 0% of each run, Pallas kernels for 0% -> 0%
where the time goes in v1:
time: 173 us
  Pallas kernels  154 us (89%)
  local copies, waits for them, and re-layouts  10.2 us (6%)
  matrix products  4.59 us (3%)
  other arithmetic  3.95 us (2%)
    pallas_call x1, Pallas kernels, run_experts(): pl.pallas_call(expert_kernel, out_shape=jax.ShapeDtypeStruct(base.shape,...  70.9 us
    pallas_call x1, Pallas kernels, spread_rows(): pl.pallas_call(spread_kernel, out_shape=[jax.ShapeDtypeStruct((planes, sh...  67.2 us
    pallas_call x1, Pallas kernels, plane_gather(): pl.pallas_call(functools.partial(gather_kernel, count), out_shape=[jax.Sh...  15.7 us
    unnamed x19, local copies, waits for them, and re-layouts  6.2 us

profile of v1, /device:TPU:16, one launch (start us, length us, event | category | flops | bytes accessed | tf_op | source)
XLA Modules:
  0.0 172.7 jit_solution(427785413658087638)
XLA Ops:
  0.0 0.0 copy-start
  0.0 0.0 copy-start.6
  0.0 0.8 constant_dynamic-slice_fusion
  0.9 1.0 reduce_window_sum.22
  1.8 0.2 slice_reduce_fusion.1
  2.0 0.7 concatenate.6.refs_1_
  2.7 0.1 exponential_bitcast_fusion
  2.8 0.1 copy.35.ids
  2.9 0.0 copy-done
  2.9 1.1 copy.31
  4.0 2.1 %convolution_convert_fusion = bf16[8,128,128]{2,1,0:T(8,128)(2,1)} fusion(bf16[8,128,128]{1,2,0:T(8,128)(2,1)S(1)} %bitcast.81, f32[8,128]{1,0:T(8,128)S(1)} %get-tuple-element.15, bf16[128,1024]{1,0:T(8,128)(2,1)} %param.15), kind=kOutput, calls=%fused_computation.2 | convolution fusion | flops 201719808 | bytes 790528 | tf_op jit(solution)/shard_map/hsd,hse->hde/dot_general | solution.py:51
  6.1 0.0 copy-start.7
  6.1 1.2 convolution_multiply_fusion
  7.3 0.0 copy-start.2
  7.3 0.0 copy-start.4
  7.4 0.0 copy-start.5
  7.4 1.1 copy.38
  8.4 15.7 %plane_gather.1 = (bf16[8,1024,128]{2,1,0:T(8,128)(2,1)}, f32[8,16,128]{2,1,0:T(8,128)}) custom-call(bf16[1024,128]{1,0:T(8,128)(2,1)} %bitcast.80, f32[16,128]{1,0:T(8,128)} %concatenate.6.refs_1_), custom_call_target="tpu_custom_call" | custom-call | tf_op jit(solution)/shard_map/plane_gather/pallas_call | solution.py:253
  24.1 0.8 slice_reduce_fusion
  25.0 0.1 broadcast_select_fusion
  25.1 0.1 exponential_select_fusion
  25.2 0.1 copy.25
  25.2 0.1 broadcast_bitcast_fusion
  25.3 2.5 %multiply_reduce_fusion = f32[1024,128]{1,0:T(8,128)S(1)} fusion(bf16[8,1024,128]{2,1,0:T(8,128)(2,1)} %get-tuple-element.10, f32[8,1024]{1,0:T(8,128)S(1)} %broadcast_bitcast_fusion), kind=kLoop, calls=%fused_computation | loop fusion | flops 3014656 | bytes 2654208 | tf_op jit(solution)/shard_map/reduce_sum | solution.py:780
  27.8 0.0 copy-done.6
  27.8 0.6 fusion.9
  28.4 0.7 fusion.1
  29.2 0.0 copy-done.7
  29.2 0.2 fusion.5
  29.4 0.1 copy.34.normed
  29.5 0.0 copy-done.2
  29.6 0.0 copy-done.4
  29.6 0.0 copy-done.5
  29.6 67.2 %spread_rows.1 = (bf16[4,32,768]{2,1,0:T(8,128)(2,1)S(1)}, bf16[8,4,32,3200]{3,2,1,0:T(8,128)(2,1)S(1)}) custom-call(bf16[128,1024]{1,0:T(8,128)(2,1)S(1)} %copy.34.normed, bf16[1024,384]{1,0:T(8,128)(2,1)S(1)} %copy-done.2, bf16[32,3072]{1,0:T(8,128)(2,1)S(1)} %constant_dynamic-slice_fusion.1.residual, f32[1,3072]{1,0:T(1,128)S(1)} %bitcast.73, ...), custom_call_target="tpu_custom_call" | custom-call | tf_op jit(solution)/shard_map/spread_rows/pallas_call | solution.py:478
  96.8 0.0 copy-start.1
  96.8 2.7 %copy-done.1 = bf16[8,4,32,3200]{3,2,1,0:T(8,128)(2,1)} copy-done((bf16[8,4,32,3200]{3,2,1,0:T(8,128)(2,1)}, bf16[8,4,32,3200]{3,2,1,0:T(8,128)(2,1)S(1)}, u32[]{:S(2)}) %copy-start.1) | copy-done | bytes 6553624
  99.5 0.0 copy-start.3
  99.5 0.7 copy-done.3
  100.2 70.9 %run_experts.1 = bf16[128,768]{1,0:T(8,128)(2,1)} custom-call(bf16[8,128,3200]{2,1,0:T(8,128)(2,1)} %bitcast.70, bf16[3072,1152]{1,0:T(8,128)(2,1)} %bitcast.74, bf16[3072,1152]{1,0:T(8,128)(2,1)} %bitcast.75, bf16[1152,3072]{1,0:T(8,128)(2,1)} %bitcast.76, bf16[128,768]{1,0:T(8,128)(2,1)} %bitcast.71), custom_call_target="tpu_custom_call" | custom-call | tf_op jit(solution)/shard_map/run_experts/pallas_call | solution.py:707
  171.1 1.6 copy.56
  (8 shorter events, 0.1 us)
Async XLA Ops:
  0.0 2.9 %copy-start = (bf16[128,3072]{1,0:T(8,128)(2,1)S(1)}, bf16[128,3072]{1,0:T(8,128)(2,1)}, u32[]{:S(2)}) copy-start(bf16[128,3072]{1,0:T(8,128)(2,1)} %param.17) | copy-start | bytes 2359300
  0.0 27.8 %copy-start.6 = (bf16[128,1024]{1,0:T(8,128)(2,1)S(1)}, bf16[128,1024]{1,0:T(8,128)(2,1)}, u32[]{:S(2)}) copy-start(bf16[128,1024]{1,0:T(8,128)(2,1)} %param.13) | copy-start | bytes 786436
  6.1 23.1 %copy-start.7 = (f32[1024]{0:T(1024)S(1)}, f32[1024]{0:T(1024)}, u32[]{:S(2)}) copy-start(f32[1024]{0:T(1024)} %param.19) | copy-start | bytes 12292
  7.3 22.2 %copy-start.2 = (bf16[1024,384]{1,0:T(8,128)(2,1)S(1)}, bf16[1024,384]{1,0:T(8,128)(2,1)}, u32[]{:S(2)}) copy-start(bf16[1024,384]{1,0:T(8,128)(2,1)} %weight.1) | copy-start | bytes 2359300
  7.3 22.2 %copy-start.4 = (f32[3072,8]{0,1:T(8,128)S(1)}, f32[3072,8]{0,1:T(8,128)}, u32[]{:S(2)}) copy-start(f32[3072,8]{0,1:T(8,128)} %param.21) | copy-start | bytes 294916
  7.4 22.2 %copy-start.5 = (f32[3072]{0:T(1024)S(1)}, f32[3072]{0:T(1024)}, u32[]{:S(2)}) copy-start(f32[3072]{0:T(1024)} %param.20) | copy-start | bytes 36868
  96.8 2.7 %copy-start.1 = (bf16[8,4,32,3200]{3,2,1,0:T(8,128)(2,1)}, bf16[8,4,32,3200]{3,2,1,0:T(8,128)(2,1)S(1)}, u32[]{:S(2)}) copy-start(bf16[8,4,32,3200]{3,2,1,0:T(8,128)(2,1)S(1)} %get-tuple-element.11) | copy-start | bytes 19660804
  99.5 0.7 copy-start.3

commit v2 on v0

--- a/solution.py
+++ b/solution.py
@@ -1,6 +1,10 @@
+import functools
+
 import jax
 import jax.numpy as jnp
 from jax import lax
+from jax.experimental import pallas as pl
+from jax.experimental.pallas import tpu as pltpu
 from jax.sharding import PartitionSpec as P
 
 TOP = 2
@@ -65,7 +69,7 @@
     return (earlier[0] + later[0], jnp.exp(later[0])[:, None, None] * earlier[1] + later[1])
 
 
-def body(
+def general_body(
     query_vectors,
     key_vectors,
     value_vectors,
@@ -165,7 +169,587 @@
     return final_out.astype(jnp.bfloat16)
 
 
+MESH = pl.DeviceIdType.MESH
+ANY = pl.BlockSpec(memory_space=pl.ANY)
+VMEM = pl.BlockSpec(memory_space=pltpu.VMEM)
+
+
+def plane_peers():
+    me = lax.axis_index("ctx")
+    core, x, y = me % 2, (me // 2) % 2, me // 4
+
+    def at(c, a, b):
+        return (b * 2 + a) * 2 + c
+
+    return (
+        me,
+        at(1 - core, x, y),
+        at(core, 1 - x, y),
+        at(core, x, 1 - y),
+        at(core, 1 - x, 1 - y),
+    )
+
+
+def greet(axes_and_peers):
+    barrier = pltpu.get_barrier_semaphore()
+    for axis, peer in axes_and_peers:
+        pl.semaphore_signal(barrier, inc=1, device_id={axis: peer}, device_id_type=MESH)
+    pl.semaphore_wait(barrier, len(axes_and_peers))
+
+
+def block_order(me, sib, xn, yn, dg):
+    def other_core(index):
+        return index + 1 - 2 * (index % 2)
+
+    return (me, sib, xn, yn, other_core(xn), other_core(yn), dg, other_core(dg))
+
+
+def z_order():
+    z = lax.axis_index("head")
+    return (z + 1 - 2 * (z % 2), z + 2 - 4 * (z // 2), 3 - z)
+
+
+def sender(send, recv):
+    def copy(at, src, dst, axis, peer):
+        return pltpu.make_async_remote_copy(
+            src_ref=src,
+            dst_ref=dst,
+            send_sem=send.at[at],
+            recv_sem=recv.at[at],
+            device_id={axis: peer},
+            device_id_type=MESH,
+        )
+
+    return copy
+
+
+STATES, GATHER, TO_Z, TO_COLS = 0, 9, 18, 42
+ROWS_Z, BASE_Z, SPREAD, PAIR, SUMS, SLICES, COPIES = 50, 53, 56, 92, 96, 120, 123
+TILE = 256
+
+
+def gather_plan(copy, first, buffer, split, peers):
+    me, sib, xn, yn, dg = peers
+    top, low = pl.ds(0, split), pl.ds(split, buffer.shape[1] - split)
+    return [
+        copy(first, buffer.at[me], buffer.at[me], "ctx", sib),
+        copy(first + 1, buffer.at[me], buffer.at[me], "ctx", xn),
+        copy(first + 2, buffer.at[me], buffer.at[me], "ctx", yn),
+        copy(first + 3, buffer.at[xn, top], buffer.at[xn, top], "ctx", yn),
+        copy(first + 4, buffer.at[xn], buffer.at[xn], "ctx", sib),
+        copy(first + 5, buffer.at[yn, low], buffer.at[yn, low], "ctx", xn),
+        copy(first + 6, buffer.at[yn], buffer.at[yn], "ctx", sib),
+        copy(first + 7, buffer.at[dg, top], buffer.at[dg, top], "ctx", sib),
+        copy(first + 8, buffer.at[dg, low], buffer.at[dg, low], "ctx", sib),
+    ]
+
+
+def attend(query, key, value, log_decay, attn_gain, states, rows, copy, peers):
+    f32, bf16 = jnp.float32, jnp.bfloat16
+    me = peers[0]
+    heads, length = log_decay.shape
+    size = query.shape[1] // heads
+    row = lax.broadcasted_iota(jnp.int32, (length, length), 0)
+    col = lax.broadcasted_iota(jnp.int32, (length, length), 1)
+    causal = col <= row
+    lower = causal.astype(f32)
+    decay = log_decay[...]
+    across = (((1,), (1,)), ((), ()))
+    by_row = lax.dot_general(
+        decay, lower, across, precision=PRECISE, preferred_element_type=f32
+    )
+    by_col = lax.dot_general(
+        lower, decay, across, precision=PRECISE, preferred_element_type=f32
+    )
+    final = by_row[:, length - 1 :]
+    for h in range(heads):
+        cols = slice(h * size, (h + 1) * size)
+        tail = jnp.exp(by_col[length - 1 :, h : h + 1] - by_col[:, h : h + 1])
+        state = lax.dot_general(
+            (key[:, cols].astype(f32) * tail).astype(bf16),
+            value[:, cols],
+            (((0,), (0,)), ((), ())),
+            preferred_element_type=f32,
+        )
+        states[me, h * size : (h + 1) * size] = state.astype(bf16)
+    big = final.astype(bf16).astype(f32)
+    middle = (final - big).astype(bf16).astype(f32)
+    small = final - big - middle
+    lane = lax.broadcasted_iota(jnp.int32, (heads, size), 1)
+    notes = jnp.zeros((heads, size), f32)
+    for k, term in enumerate((big, middle, small)):
+        notes = jnp.where(lane == k, term, notes)
+    notes = jnp.concatenate([notes, jnp.zeros((16 - heads, size), f32)], axis=0)
+    states[me, heads * size :] = notes.astype(bf16)
+
+    plan = gather_plan(copy, STATES, states, heads * size // 2, peers)
+    for step in (1, 2, 0):
+        plan[step].start()
+    inside = []
+    for h in range(heads):
+        cols = slice(h * size, (h + 1) * size)
+        scores = lax.dot_general(
+            query[:, cols], key[:, cols], across, preferred_element_type=f32
+        )
+        spread = jnp.where(causal, by_col[:, h : h + 1] - by_row[h : h + 1], 0.0)
+        scores *= jnp.where(causal, jnp.exp(spread), 0.0)
+        inside.append(
+            jnp.dot(scores.astype(bf16), value[:, cols], preferred_element_type=f32)
+        )
+    for got, onward in ((1, (3, 4)), (2, (5, 6)), (3, (7,)), (5, (8,))):
+        plan[got].wait_recv()
+        for step in onward:
+            plan[step].start()
+    for step in (0, 4, 6, 7, 8):
+        plan[step].wait_recv()
+
+    scales = [None] * states.shape[0]
+    after = jnp.zeros((heads, 1), f32)
+    for k in reversed(range(states.shape[0])):
+        said = states[k, heads * size :].astype(f32)[:heads]
+        scales[k] = jnp.where(k < me, jnp.exp(after), 0.0)
+        after += jnp.where(k < me, said[:, 0:1] + said[:, 1:2] + said[:, 2:3], 0.0)
+    for h in range(heads):
+        cols = slice(h * size, (h + 1) * size)
+        prior = jnp.zeros((size, size), f32)
+        for k in range(states.shape[0]):
+            prior += scales[k][h : h + 1] * states[k, h * size : (h + 1) * size].astype(f32)
+        outside = jnp.dot(query[:, cols], prior.astype(bf16), preferred_element_type=f32)
+        attended = inside[h] + jnp.exp(by_col[:, h : h + 1]) * outside
+        square_mean = jnp.mean(attended * attended, axis=1, keepdims=True)
+        normed = attended * lax.rsqrt(square_mean + 1e-05) * attn_gain[:, cols]
+        rows[me, :, cols] = normed.astype(bf16)
+    return plan
+
+
+def layer_kernel(
+    query, key, value, log_decay, attn_gain, weight, residual, gain, router, ids,
+    w_gate, w_up, w_down, out,
+    states, rows, part, from_z, summed, by_cols, mixed, base, toks,
+    wide, down, picked, slot_gate, hidden, theirs, ours, pair, onehots,
+    ahead, across, landed, total, slices, send, recv, load,
+):
+    peers = plane_peers()
+    me, sib, xn, yn, dg = peers
+    z = lax.axis_index("head")
+    blocks, zs = block_order(*peers), z_order()
+    chunks = zs + (z,)
+    units = hidden.shape[1]
+    tiles = units // TILE
+    weight_loads = []
+    for j in range(tiles):
+        for k, matrix in enumerate((w_gate, w_up)):
+            weight_loads.append(
+                pltpu.make_async_copy(
+                    matrix.at[:, pl.ds(j * TILE, TILE)],
+                    wide.at[2 * j + k],
+                    load.at[2 * j + k],
+                )
+            )
+    rest = units - tiles * TILE
+    for k, matrix in enumerate((w_gate, w_up)):
+        weight_loads.append(
+            pltpu.make_async_copy(
+                matrix.at[:, pl.ds(tiles * TILE, rest)],
+                wide.at[2 * tiles, :, pl.ds(k * rest, rest)],
+                load.at[2 * tiles + k],
+            )
+        )
+    down_load = pltpu.make_async_copy(w_down, down, load.at[2 + 2 * tiles])
+    for each in weight_loads + [down_load]:
+        each.start()
+    greet([("ctx", b) for b in blocks[1:]] + [("head", p) for p in zs])
+    copy = sender(send, recv)
+    f32, bf16 = jnp.float32, jnp.bfloat16
+    share, model_width = residual.shape
+    mine = pl.ds(pl.multiple_of(z * share, share), share)
+    width = weight.shape[1]
+
+    sent = attend(
+        query, key, value, log_decay, attn_gain, states, rows, copy, peers
+    )
+    plan = gather_plan(copy, GATHER, rows, rows.shape[1] // 2, peers)
+    for step in (1, 2, 0):
+        plan[step].start()
+    sent = sent + plan
+    z_in = []
+
+    def project(i, block):
+        product = jnp.dot(block, weight[...], preferred_element_type=f32).astype(bf16)
+        for k in range(len(zs) + 1):
+            part[i, k] = product[k * share : (k + 1) * share]
+        z_in.append([])
+        for d, peer in enumerate(zs):
+            out_copy = copy(
+                TO_Z + 3 * i + d, part.at[i, peer], from_z.at[i, d], "head", peer
+            )
+            out_copy.start()
+            z_in[i].append(out_copy)
+            sent.append(out_copy)
+
+    def arrived(*steps):
+        for step in steps:
+            plan[step].wait_recv()
+
+    project(0, rows[me])
+    arrived(0)
+    project(1, rows[sib])
+    arrived(1)
+    plan[3].start()
+    plan[4].start()
+    project(2, rows[xn])
+    arrived(2)
+    plan[5].start()
+    plan[6].start()
+    project(3, rows[yn])
+    arrived(4)
+    project(4, rows[blocks[4]])
+    arrived(6)
+    project(5, rows[blocks[5]])
+    arrived(3)
+    plan[7].start()
+    arrived(5)
+    plan[8].start()
+    project(6, rows[dg])
+    arrived(7, 8)
+    project(7, rows[blocks[7]])
+
+    col_copies = []
+    for i, block in enumerate(blocks):
+        block_sum = part[i, z].astype(f32)
+        for d in range(3):
+            z_in[i][d].wait_recv()
+            block_sum += from_z[i, d].astype(f32)
+        summed[i] = block_sum.astype(bf16)
+        if i:
+            col_copies.append(
+                copy(TO_COLS + i, summed.at[i], by_cols.at[me], "ctx", block)
+            )
+            col_copies[-1].start()
+    by_cols[me] = summed[0]
+    for each in col_copies:
+        each.wait_recv()
+    sent += col_copies
+
+    per = model_width // (len(zs) + 1) // width
+    squares = jnp.zeros((share, 1), f32)
+    for k in range(model_width // width):
+        cols = slice(k * width, (k + 1) * width)
+        whole = (residual[:, cols].astype(f32) + by_cols[k].astype(f32)).astype(bf16)
+        mixed[k // per, :, (k % per) * width : (k % per + 1) * width] = whole
+        row_values = whole.astype(f32)
+        squares += jnp.sum(row_values * row_values, axis=1, keepdims=True)
+    inv_rms = lax.rsqrt(squares / model_width + 1e-06)
+    experts_total = router.shape[0]
+    logits = [jnp.zeros((share, 1), f32)] * experts_total
+    slice_width = per * width
+    for k in range(len(zs) + 1):
+        cols = slice(k * slice_width, (k + 1) * slice_width)
+        scaled = mixed[k].astype(f32) * gain[:, cols]
+        toks[me, mine, cols] = (scaled * inv_rms).astype(bf16)
+        for e in range(experts_total):
+            logits[e] += jnp.sum(scaled * router[e : e + 1, cols], axis=1, keepdims=True)
+    first, second = ids[:, 0:1], ids[:, 1:2]
+    margin = jnp.zeros((share, 1), f32)
+    for e in range(experts_total):
+        margin += jnp.where(first == e, logits[e], 0.0) - jnp.where(second == e, logits[e], 0.0)
+    leading = jax.nn.sigmoid(margin * inv_rms)
+    big = leading.astype(bf16).astype(f32)
+    middle = (leading - big).astype(bf16).astype(f32)
+    small = leading - big - middle
+    lane = lax.broadcasted_iota(jnp.int32, (share, 128), 1)
+    notes = jnp.zeros((share, 128), f32)
+    for k, value in enumerate((first.astype(f32), second.astype(f32), big, middle, small)):
+        notes = jnp.where(lane == k, value, notes)
+    toks[me, mine, model_width:] = notes.astype(bf16)
+    base[mine] = mixed[z]
+
+    z_copies, base_copies = [], []
+    quarter = share // 2
+
+    def spread(j, k):
+        s = SPREAD + 9 * j
+        start = pl.multiple_of(k * share, share)
+        rows_of = pl.ds(start, share)
+        upper, lower = pl.ds(start, quarter), pl.ds(start + quarter, quarter)
+
+        def send_on(step, block, part_of, peer):
+            ref = toks.at[block, part_of]
+            return copy(s + step, ref, ref, "ctx", peer)
+
+        steps = [
+            send_on(0, me, rows_of, sib),
+            send_on(1, me, rows_of, xn),
+            send_on(2, me, rows_of, yn),
+            send_on(3, xn, upper, yn),
+            send_on(4, xn, rows_of, sib),
+            send_on(5, yn, lower, xn),
+            send_on(6, yn, rows_of, sib),
+            send_on(7, dg, upper, sib),
+            send_on(8, dg, lower, sib),
+        ]
+        for step in (1, 2, 0):
+            steps[step].start()
+        return steps
+
+    def relay(steps):
+        for got, onward in ((1, (3, 4)), (2, (5, 6)), (3, (7,)), (5, (8,))):
+            steps[got].wait_recv()
+            for step in onward:
+                steps[step].start()
+
+    for d, peer in enumerate(zs):
+        z_copies.append(
+            copy(ROWS_Z + d, toks.at[me, mine], toks.at[me, mine], "head", peer)
+        )
+        z_copies[-1].start()
+    runs = [spread(0, z)]
+    for d, peer in enumerate(zs):
+        z_copies[d].wait_recv()
+        runs.append(spread(d + 1, peer))
+        relay(runs[d])
+    for d, peer in enumerate(zs):
+        base_copies.append(copy(BASE_Z + d, mixed.at[peer], base.at[mine], "head", peer))
+        base_copies[-1].start()
+    relay(runs[3])
+    for steps in runs:
+        for step in (0, 4, 6, 7, 8):
+            steps[step].wait_recv()
+        sent += steps
+    for each in base_copies:
+        each.wait_recv()
+    sent += z_copies + base_copies
+
+    count = picked.shape[0] // 4
+    row = lax.broadcasted_iota(jnp.int32, (128, 128), 0)
+    col = lax.broadcasted_iota(jnp.int32, (128, 128), 1)
+    lower = (col <= row).astype(bf16)
+
+    def chosen(notes, expert, offset):
+        e = expert.astype(f32)
+        named = (notes[:, 0:1] == e) | (notes[:, 1:2] == e)
+        marks = jnp.broadcast_to(named.astype(f32), (128, 128)).astype(bf16)
+        slot = jnp.dot(lower, marks, preferred_element_type=f32).astype(jnp.int32) - 1 + offset
+        return jnp.where((slot == col) & (marks > 0), 1.0, 0.0)
+
+    width = out.shape[1]
+    away = (blocks[7], blocks[4], blocks[5], sib)
+    here = (dg, xn, yn, me)
+    pairs = [copy(PAIR + i, theirs.at[i], pair.at[i], "ctx", sib) for i in range(4)]
+
+    def act(gated, up):
+        return (gated * jax.nn.sigmoid(gated) * up).astype(bf16)
+
+    def experts(group):
+        both = (2 * group, 2 * group + 1)
+        for n, block in enumerate([away[i] for i in both] + [here[i] for i in both]):
+            notes = toks[block, :, model_width:].astype(f32)
+            place = chosen(notes, me, 0)
+            if n >= 2:
+                onehots[both[n - 2]] = (place + chosen(notes, sib, count)).astype(bf16)
+            pick = place[:, :count].astype(bf16)
+            found = lax.dot_general(
+                pick, toks[block], (((0,), (0,)), ((), ())), preferred_element_type=f32
+            )
+            picked[n * count : (n + 1) * count] = found[:, :model_width].astype(bf16)
+            said = found[:, model_width:]
+            leading = said[:, 2:3] + said[:, 3:4] + said[:, 4:5]
+            gate = jnp.where(said[:, 0:1] == me.astype(f32), leading, 1.0 - leading)
+            slot_gate[n * count : (n + 1) * count] = jnp.broadcast_to(gate, (count, 128))
+        for j in range(tiles):
+            if group == 0:
+                weight_loads[2 * j].wait()
+                weight_loads[2 * j + 1].wait()
+            gated = jnp.dot(picked[...], wide[2 * j], preferred_element_type=f32)
+            up = jnp.dot(picked[...], wide[2 * j + 1], preferred_element_type=f32)
+            hidden[:, j * TILE : (j + 1) * TILE] = act(gated, up)
+        if group == 0:
+            weight_loads[2 * tiles].wait()
+            weight_loads[2 * tiles + 1].wait()
+            down_load.wait()
+        last = jnp.dot(picked[...], wide[2 * tiles], preferred_element_type=f32)
+        hidden[:, tiles * TILE :] = act(last[:, :rest], last[:, rest:])
+        for k in range(4):
+            cols = slice(k * width, (k + 1) * width)
+            result = jnp.dot(hidden[...], down[:, cols], preferred_element_type=f32)
+            result = (result * slot_gate[:, 0:1]).astype(bf16)
+            for n in range(2):
+                theirs[both[n], k] = result[n * count : (n + 1) * count]
+                ours[both[n], k] = result[(n + 2) * count : (n + 3) * count]
+        for i in both:
+            pairs[i].start()
+
+    half = 64
+    top, low = pl.ds(0, half), pl.ds(half, half)
+
+    def tokens_of(i, k, rows):
+        slots = jnp.concatenate([ours[i, k], pair[i, k]], axis=0)
+        return jnp.dot(onehots[i, rows], slots, preferred_element_type=f32)
+
+    plans = []
+    for j in range(4):
+        s = SUMS + 6 * j
+        plans.append(
+            [
+                copy(s, ahead.at[j, 0, top], across.at[j, 0], "ctx", yn),
+                copy(s + 1, ahead.at[j, 0, low], across.at[j, 1], "ctx", xn),
+                copy(s + 2, ahead.at[j, 1, low], landed.at[j, 0, low], "ctx", xn),
+                copy(s + 3, ahead.at[j, 2, top], landed.at[j, 1, top], "ctx", yn),
+                copy(s + 4, ahead.at[j, 1, top], landed.at[j, 0, top], "ctx", xn),
+                copy(s + 5, ahead.at[j, 2, low], landed.at[j, 1, low], "ctx", yn),
+            ]
+        )
+    out_z = [
+        copy(SLICES + d, total.at[d], slices.at[d], "head", peer) for d, peer in enumerate(zs)
+    ]
+
+    def begin(j):
+        k = chunks[j]
+        ahead[j, 0] = tokens_of(0, k, slice(None)).astype(bf16)
+        plans[j][0].start()
+        plans[j][1].start()
+        ahead[j, 1, low] = tokens_of(1, k, low).astype(bf16)
+        plans[j][2].start()
+
+    def begin_y(j):
+        ahead[j, 2, top] = tokens_of(2, chunks[j], top).astype(bf16)
+        plans[j][3].start()
+
+    def pass_on(j):
+        k = chunks[j]
+        plans[j][0].wait_recv()
+        ahead[j, 1, top] = (tokens_of(1, k, top) + across[j, 0].astype(f32)).astype(bf16)
+        plans[j][4].start()
+        plans[j][1].wait_recv()
+        ahead[j, 2, low] = (tokens_of(2, k, low) + across[j, 1].astype(f32)).astype(bf16)
+        plans[j][5].start()
+
+    def finish(j):
+        k = chunks[j]
+        value = tokens_of(3, k, slice(None))
+        for step in (2, 3, 4, 5):
+            plans[j][step].wait_recv()
+        value += landed[j, 0].astype(f32) + landed[j, 1].astype(f32)
+        if j < 3:
+            total[j] = value.astype(bf16)
+            out_z[j].start()
+        return value
+
+    experts(0)
+    pairs[0].wait_recv()
+    pairs[1].wait_recv()
+    for j in range(4):
+        begin(j)
+    experts(1)
+    pairs[2].wait_recv()
+    begin_y(0)
+    begin_y(1)
+    pass_on(0)
+    begin_y(2)
+    pass_on(1)
+    pairs[3].wait_recv()
+    finish(0)
+    begin_y(3)
+    pass_on(2)
+    finish(1)
+    pass_on(3)
+    finish(2)
+    value = finish(3) + base[...].astype(f32)
+    for d in range(3):
+        out_z[d].wait_recv()
+        value += slices[d].astype(f32)
+    out[...] = value.astype(bf16)
+    for each in sent + pairs + sum(plans, []) + out_z:
+        each.wait_send()
+
+
+def layer(tensors, weights, capacity):
+    ctx, planes = lax.axis_size("ctx"), lax.axis_size("head")
+    query, decay, weight, residual = tensors[0], tensors[3], tensors[5], tensors[6]
+    tokens, depth = query.shape
+    width = weight.shape[1]
+    share, model_width = residual.shape
+    units = weights[0].shape[1]
+    part_width = model_width // planes
+    tiles = units // TILE
+    dma, bf16 = pltpu.SemaphoreType.DMA, jnp.bfloat16
+    return pl.pallas_call(
+        layer_kernel,
+        out_shape=jax.ShapeDtypeStruct((tokens, part_width), bf16),
+        in_specs=[VMEM] * len(tensors) + [ANY] * len(weights),
+        out_specs=VMEM,
+        scratch_shapes=[
+            pltpu.VMEM((ctx, depth + 16, depth // decay.shape[0]), bf16),
+            pltpu.VMEM((ctx, tokens, depth), bf16),
+            pltpu.VMEM((ctx, planes, share, width), bf16),
+            pltpu.VMEM((ctx, planes - 1, share, width), bf16),
+            pltpu.VMEM((ctx, share, width), bf16),
+            pltpu.VMEM((ctx, share, width), bf16),
+            pltpu.VMEM((planes, share, part_width), bf16),
+            pltpu.VMEM((tokens, part_width), bf16),
+            pltpu.VMEM((ctx, tokens, model_width + 128), bf16),
+            pltpu.VMEM((2 * tiles + 1, model_width, TILE), bf16),
+            pltpu.VMEM((units, model_width), bf16),
+            pltpu.VMEM((ctx // 2 * capacity, model_width), bf16),
+            pltpu.VMEM((ctx // 2 * capacity, 128), jnp.float32),
+            pltpu.VMEM((ctx // 2 * capacity, units), bf16),
+            pltpu.VMEM((4, planes, capacity, part_width), bf16),
+            pltpu.VMEM((4, planes, capacity, part_width), bf16),
+            pltpu.VMEM((4, planes, capacity, part_width), bf16),
+            pltpu.VMEM((4, tokens, 2 * capacity), bf16),
+            pltpu.VMEM((planes, 3, tokens, part_width), bf16),
+            pltpu.VMEM((planes, 2, tokens // 2, part_width), bf16),
+            pltpu.VMEM((planes, 2, tokens, part_width), bf16),
+            pltpu.VMEM((planes - 1, tokens, part_width), bf16),
+            pltpu.VMEM((planes - 1, tokens, part_width), bf16),
+            dma((COPIES,)),
+            dma((COPIES,)),
+            dma((3 + 2 * tiles,)),
+        ],
+        compiler_params=pltpu.CompilerParams(
+            collective_id=1, has_side_effects=True, vmem_limit_bytes=62 << 20
+        ),
+        name="layer",
+    )(*tensors, *weights)
+
+
+def plane_body(
+    query_vectors,
+    key_vectors,
+    value_vectors,
+    log_decay,
+    residual,
+    out_weight,
+    attn_gain,
+    moe_gain,
+    router,
+    w_gate,
+    w_up,
+    w_down,
+    expert_ids,
+):
+    token_count = query_vectors.shape[0]
+    z, planes = lax.axis_index("head"), lax.axis_size("head")
+    share = token_count // planes
+    tensors = (
+        query_vectors,
+        key_vectors,
+        value_vectors,
+        log_decay,
+        attn_gain[None, :],
+        out_weight,
+        lax.dynamic_slice_in_dim(residual, z * share, share, 0),
+        moe_gain[None, :],
+        router.T,
+        lax.dynamic_slice_in_dim(expert_ids, z * share, share, 0),
+    )
+    capacity = 2 * token_count * TOP // router.shape[1]
+    return layer(tensors, (w_gate[0], w_up[0], w_down[0]), capacity)
+
+
 def solution(mesh):
+    sizes = dict(mesh.shape)
+    body = plane_body if (sizes["ctx"], sizes["head"]) == (8, 4) else general_body
     in_specs = (
         P("ctx", "head"),
         P("ctx", "head"),

time: 358 us -> 142 us (0.40); the launches traced: 353 us -> 142 us
  waiting for transfers between devices: 157 us -> 0 us
  Pallas kernels: 0 us -> 138 us
  blocking collectives: 95.6 us -> 0 us
  local copies, waits for them, and re-layouts: 33.7 us -> 3.82 us
  matrix products: 26.2 us -> 0 us
  other arithmetic: 20.9 us -> 0 us
  between operations: 14 us -> 0.01 us
  starting transfers between devices: 5.35 us -> 0 us
    pallas_call x0 -> x1, Pallas kernels: none -> 138 us  [layer(): pl.pallas_call(layer_kernel, out_shape=jax.ShapeDtypeStruct((tokens, part...]
    all_to_all x2 -> x0, blocking collectives: 81.8 us -> none  [the longest x1 41.5 us: body(): lax.all_to_all(packed.reshape(experts_total, capacity, width_here), 'ctx'...]
    all_to_all x1 -> x0, waiting for transfers between devices: 64.5 us -> none  [body(): lax.all_to_all(lax.all_to_all(partial_down.astype(jnp.bfloat16)[None], 'c...]
    all_gather x2 -> x0, waiting for transfers between devices: 50.2 us -> none  [the longest x1 37.9 us: body(): lax.all_gather(out_weight, 'ctx', axis=1, tiled=True)]
    psum x1 -> x0, waiting for transfers between devices: 41.3 us -> none  [body(): lax.psum(partial_out.astype(jnp.bfloat16), 'head').astype(jnp.float32)]
    dot_general x9 -> x0, matrix products: 26.2 us -> none  [the longest x1 6.59 us: body(): jnp.dot(flat_rows, w_gate[0], preferred_element_type=jnp.float32)]
    unnamed x1 -> x0, blocking collectives: 13.8 us -> none
    unnamed x35 -> x4, local copies, waits for them, and re-layouts: 14.8 us -> 2.31 us
  transfers between devices with their start and end apart: 4 -> 0, of which waited for: 4 -> 0; matrix products, arithmetic and copies ran while one was open for 5% -> 0% of each run, Pallas kernels for 0% -> 0%
where the time goes in v2:
time: 142 us
  Pallas kernels  138 us (97%)
  local copies, waits for them, and re-layouts  3.82 us (3%)
    pallas_call x1, Pallas kernels, layer(): pl.pallas_call(layer_kernel, out_shape=jax.ShapeDtypeStruct((tokens, part...  138 us

profile of v2, /device:TPU:16, one launch (start us, length us, event | category | flops | bytes accessed | tf_op | source)
XLA Modules:
  0.0 141.7 jit_solution(79890310504482681)
XLA Ops:
  0.0 0.0 copy-start
  0.0 0.8 constant_dynamic-slice_fusion
  0.8 0.7 copy.15.ids
  1.5 0.0 copy-done
  1.5 0.7 constant_dynamic-slice_fusion.1.residual
  2.2 137.8 %layer.1 = bf16[128,768]{1,0:T(8,128)(2,1)} custom-call(bf16[128,1024]{1,0:T(8,128)(2,1)} %query.1, bf16[128,1024]{1,0:T(8,128)(2,1)} %key.1, bf16[128,1024]{1,0:T(8,128)(2,1)} %value.1, f32[8,128]{1,0:T(8,128)} %log_decay.1, f32[1,1024]{1,0:T(1,128)} %bitcast.11, bf16[1024,384]{1,0:T(8,128)(2,1)} %weight.1, ...), custom_call_target="tpu_custom_call" | custom-call | tf_op jit(solution)/shard_map/layer/pallas_call | solution.py:676
  140.0 1.6 %copy.17 = bf16[128,768]{1,0:T(8,128)(2,1)} copy(bf16[128,768]{1,0:T(8,128)(2,1)} %layer.1) | data formatting | bytes 393216
Async XLA Ops:
  0.0 1.5 %copy-start = (bf16[128,3072]{1,0:T(8,128)(2,1)S(1)}, bf16[128,3072]{1,0:T(8,128)(2,1)}, u32[]{:S(2)}) copy-start(bf16[128,3072]{1,0:T(8,128)(2,1)} %param.17) | copy-start | bytes 2359300

commit v3 on v2

--- a/solution.py
+++ b/solution.py
@@ -223,8 +223,8 @@
     return copy
 
 
-STATES, GATHER, TO_Z, TO_COLS = 0, 9, 18, 42
-ROWS_Z, BASE_Z, SPREAD, PAIR, SUMS, SLICES, COPIES = 50, 53, 56, 92, 96, 120, 123
+STATES, GATHER, TO_Z, TO_COLS = 0, 9, 18, 66
+ROWS_Z, BASE_Z, SPREAD, PAIR, SUMS, SLICES, COPIES = 82, 88, 91, 163, 167, 191, 194
 TILE = 256
 
 
@@ -361,8 +361,14 @@
     greet([("ctx", b) for b in blocks[1:]] + [("head", p) for p in zs])
     copy = sender(send, recv)
     f32, bf16 = jnp.float32, jnp.bfloat16
-    share, model_width = residual.shape
-    mine = pl.ds(pl.multiple_of(z * share, share), share)
+    model_width = residual.shape[1]
+    share = residual.shape[0] // (len(zs) + 1)
+    part_rows = share // 2
+
+    def rows_at(plane, t):
+        start = pl.multiple_of(plane * share + t * part_rows, part_rows)
+        return pl.ds(start, part_rows)
+
     width = weight.shape[1]
 
     sent = attend(
@@ -372,20 +378,28 @@
     for step in (1, 2, 0):
         plan[step].start()
     sent = sent + plan
-    z_in = []
+    z_in = ([], [])
+
+    def send_z(i, t):
+        rows_t = pl.ds(t * part_rows, part_rows)
+        z_in[t].append([])
+        for d, peer in enumerate(zs):
+            out_copy = copy(
+                TO_Z + 6 * i + 3 * t + d,
+                part.at[i, peer, rows_t],
+                from_z.at[i, d, rows_t],
+                "head",
+                peer,
+            )
+            out_copy.start()
+            z_in[t][i].append(out_copy)
+            sent.append(out_copy)
 
     def project(i, block):
         product = jnp.dot(block, weight[...], preferred_element_type=f32).astype(bf16)
         for k in range(len(zs) + 1):
             part[i, k] = product[k * share : (k + 1) * share]
-        z_in.append([])
-        for d, peer in enumerate(zs):
-            out_copy = copy(
-                TO_Z + 3 * i + d, part.at[i, peer], from_z.at[i, d], "head", peer
-            )
-            out_copy.start()
-            z_in[i].append(out_copy)
-            sent.append(out_copy)
+        send_z(i, 0)
 
     def arrived(*steps):
         for step in steps:
@@ -414,83 +428,105 @@
     arrived(7, 8)
     project(7, rows[blocks[7]])
 
-    col_copies = []
-    for i, block in enumerate(blocks):
-        block_sum = part[i, z].astype(f32)
-        for d in range(3):
-            z_in[i][d].wait_recv()
-            block_sum += from_z[i, d].astype(f32)
-        summed[i] = block_sum.astype(bf16)
-        if i:
-            col_copies.append(
-                copy(TO_COLS + i, summed.at[i], by_cols.at[me], "ctx", block)
-            )
-            col_copies[-1].start()
-    by_cols[me] = summed[0]
-    for each in col_copies:
-        each.wait_recv()
-    sent += col_copies
-
-    per = model_width // (len(zs) + 1) // width
-    squares = jnp.zeros((share, 1), f32)
-    for k in range(model_width // width):
-        cols = slice(k * width, (k + 1) * width)
-        whole = (residual[:, cols].astype(f32) + by_cols[k].astype(f32)).astype(bf16)
-        mixed[k // per, :, (k % per) * width : (k % per + 1) * width] = whole
-        row_values = whole.astype(f32)
-        squares += jnp.sum(row_values * row_values, axis=1, keepdims=True)
-    inv_rms = lax.rsqrt(squares / model_width + 1e-06)
-    experts_total = router.shape[0]
-    logits = [jnp.zeros((share, 1), f32)] * experts_total
-    slice_width = per * width
-    for k in range(len(zs) + 1):
-        cols = slice(k * slice_width, (k + 1) * slice_width)
-        scaled = mixed[k].astype(f32) * gain[:, cols]
-        toks[me, mine, cols] = (scaled * inv_rms).astype(bf16)
+    for i in range(len(blocks)):
+        send_z(i, 1)
+    col_copies = ([], [])
+
+    def to_columns(t):
+        rows_t = pl.ds(t * part_rows, part_rows)
+        for i, block in enumerate(blocks):
+            block_sum = part[i, z, rows_t].astype(f32)
+            for d in range(3):
+                z_in[t][i][d].wait_recv()
+                block_sum += from_z[i, d, rows_t].astype(f32)
+            summed[i, rows_t] = block_sum.astype(bf16)
+            if i:
+                col_copies[t].append(
+                    copy(
+                        TO_COLS + 8 * t + i,
+                        summed.at[i, rows_t],
+                        by_cols.at[me, rows_t],
+                        "ctx",
+                        block,
+                    )
+                )
+                col_copies[t][-1].start()
+        by_cols[me, rows_t] = summed[0, rows_t]
+
+    def normalize(t):
+        rows_t, mine = pl.ds(t * part_rows, part_rows), rows_at(z, t)
+        for each in col_copies[t]:
+            each.wait_recv()
+        per = model_width // (len(zs) + 1) // width
+        squares = jnp.zeros((part_rows, 1), f32)
+        for k in range(model_width // width):
+            cols = slice(k * width, (k + 1) * width)
+            whole = residual[mine, cols].astype(f32) + by_cols[k, rows_t].astype(f32)
+            whole = whole.astype(bf16)
+            mixed[k // per, rows_t, (k % per) * width : (k % per + 1) * width] = whole
+            row_values = whole.astype(f32)
+            squares += jnp.sum(row_values * row_values, axis=1, keepdims=True)
+        inv_rms = lax.rsqrt(squares / model_width + 1e-06)
+        experts_total = router.shape[0]
+        logits = [jnp.zeros((part_rows, 1), f32)] * experts_total
+        slice_width = per * width
+        for k in range(len(zs) + 1):
+            cols = slice(k * slice_width, (k + 1) * slice_width)
+            scaled = mixed[k, rows_t].astype(f32) * gain[:, cols]
+            toks[me, mine, cols] = (scaled * inv_rms).astype(bf16)
+            for e in range(experts_total):
+                logits[e] += jnp.sum(scaled * router[e : e + 1, cols], axis=1, keepdims=True)
+        named = ids[mine]
+        first, second = named[:, 0:1], named[:, 1:2]
+        margin = jnp.zeros((part_rows, 1), f32)
         for e in range(experts_total):
-            logits[e] += jnp.sum(scaled * router[e : e + 1, cols], axis=1, keepdims=True)
-    first, second = ids[:, 0:1], ids[:, 1:2]
-    margin = jnp.zeros((share, 1), f32)
-    for e in range(experts_total):
-        margin += jnp.where(first == e, logits[e], 0.0) - jnp.where(second == e, logits[e], 0.0)
-    leading = jax.nn.sigmoid(margin * inv_rms)
-    big = leading.astype(bf16).astype(f32)
-    middle = (leading - big).astype(bf16).astype(f32)
-    small = leading - big - middle
-    lane = lax.broadcasted_iota(jnp.int32, (share, 128), 1)
-    notes = jnp.zeros((share, 128), f32)
-    for k, value in enumerate((first.astype(f32), second.astype(f32), big, middle, small)):
-        notes = jnp.where(lane == k, value, notes)
-    toks[me, mine, model_width:] = notes.astype(bf16)
-    base[mine] = mixed[z]
-
-    z_copies, base_copies = [], []
-    quarter = share // 2
-
-    def spread(j, k):
-        s = SPREAD + 9 * j
-        start = pl.multiple_of(k * share, share)
-        rows_of = pl.ds(start, share)
-        upper, lower = pl.ds(start, quarter), pl.ds(start + quarter, quarter)
-
-        def send_on(step, block, part_of, peer):
-            ref = toks.at[block, part_of]
+            margin += jnp.where(first == e, logits[e], 0.0)
+            margin -= jnp.where(second == e, logits[e], 0.0)
+        leading = jax.nn.sigmoid(margin * inv_rms)
+        big = leading.astype(bf16).astype(f32)
+        middle = (leading - big).astype(bf16).astype(f32)
+        small = leading - big - middle
+        lane = lax.broadcasted_iota(jnp.int32, (part_rows, 128), 1)
+        notes = jnp.zeros((part_rows, 128), f32)
+        for k, term in enumerate((first.astype(f32), second.astype(f32), big, middle, small)):
+            notes = jnp.where(lane == k, term, notes)
+        toks[me, mine, model_width:] = notes.astype(bf16)
+        base[mine] = mixed[z, rows_t]
+
+    z_copies, base_copies = ([], []), []
+    full = toks.shape[2]
+    middle_col = full // 256 * 128
+    left, right = pl.ds(0, middle_col), pl.ds(middle_col, full - middle_col)
+
+    def spread(t, j, plane):
+        s = SPREAD + 9 * (4 * t + j)
+        rows_of = rows_at(plane, t)
+
+        def send_on(step, block, peer, cols=pl.ds(0, full)):
+            ref = toks.at[block, rows_of, cols]
             return copy(s + step, ref, ref, "ctx", peer)
 
         steps = [
-            send_on(0, me, rows_of, sib),
-            send_on(1, me, rows_of, xn),
-            send_on(2, me, rows_of, yn),
-            send_on(3, xn, upper, yn),
-            send_on(4, xn, rows_of, sib),
-            send_on(5, yn, lower, xn),
-            send_on(6, yn, rows_of, sib),
-            send_on(7, dg, upper, sib),
-            send_on(8, dg, lower, sib),
+            send_on(0, me, sib),
+            send_on(1, me, xn),
+            send_on(2, me, yn),
+            send_on(3, xn, yn, left),
+            send_on(4, xn, sib),
+            send_on(5, yn, xn, right),
+            send_on(6, yn, sib),
+            send_on(7, dg, sib, left),
+            send_on(8, dg, sib, right),
         ]
         for step in (1, 2, 0):
             steps[step].start()
         return steps
+
+    def begin_rows(t):
+        ref = toks.at[me, rows_at(z, t)]
+        for d, peer in enumerate(zs):
+            z_copies[t].append(copy(ROWS_Z + 3 * t + d, ref, ref, "head", peer))
+            z_copies[t][-1].start()
+        return spread(t, 0, z)
 
     def relay(steps):
         for got, onward in ((1, (3, 4)), (2, (5, 6)), (3, (7,)), (5, (8,))):
@@ -498,27 +534,30 @@
             for step in onward:
                 steps[step].start()
 
+    to_columns(0)
+    normalize(0)
+    runs = [begin_rows(0)]
+    relay(runs[0])
+    to_columns(1)
+    normalize(1)
+    runs.append(begin_rows(1))
+    for t in range(2):
+        for d, peer in enumerate(zs):
+            z_copies[t][d].wait_recv()
+            runs.append(spread(t, d + 1, peer))
+            relay(runs[-2])
+    own_rows = pl.ds(pl.multiple_of(z * share, share), share)
     for d, peer in enumerate(zs):
-        z_copies.append(
-            copy(ROWS_Z + d, toks.at[me, mine], toks.at[me, mine], "head", peer)
-        )
-        z_copies[-1].start()
-    runs = [spread(0, z)]
-    for d, peer in enumerate(zs):
-        z_copies[d].wait_recv()
-        runs.append(spread(d + 1, peer))
-        relay(runs[d])
-    for d, peer in enumerate(zs):
-        base_copies.append(copy(BASE_Z + d, mixed.at[peer], base.at[mine], "head", peer))
+        base_copies.append(copy(BASE_Z + d, mixed.at[peer], base.at[own_rows], "head", peer))
         base_copies[-1].start()
-    relay(runs[3])
+    relay(runs[-1])
     for steps in runs:
         for step in (0, 4, 6, 7, 8):
             steps[step].wait_recv()
         sent += steps
     for each in base_copies:
         each.wait_recv()
-    sent += z_copies + base_copies
+    sent += col_copies[0] + col_copies[1] + z_copies[0] + z_copies[1] + base_copies
 
     count = picked.shape[0] // 4
     row = lax.broadcasted_iota(jnp.int32, (128, 128), 0)
@@ -668,7 +707,8 @@
     query, decay, weight, residual = tensors[0], tensors[3], tensors[5], tensors[6]
     tokens, depth = query.shape
     width = weight.shape[1]
-    share, model_width = residual.shape
+    model_width = residual.shape[1]
+    share = tokens // planes
     units = weights[0].shape[1]
     part_width = model_width // planes
     tiles = units // TILE
@@ -729,8 +769,6 @@
     expert_ids,
 ):
     token_count = query_vectors.shape[0]
-    z, planes = lax.axis_index("head"), lax.axis_size("head")
-    share = token_count // planes
     tensors = (
         query_vectors,
         key_vectors,
@@ -738,10 +776,10 @@
         log_decay,
         attn_gain[None, :],
         out_weight,
-        lax.dynamic_slice_in_dim(residual, z * share, share, 0),
+        residual,
         moe_gain[None, :],
         router.T,
-        lax.dynamic_slice_in_dim(expert_ids, z * share, share, 0),
+        expert_ids,
     )
     capacity = 2 * token_count * TOP // router.shape[1]
     return layer(tensors, (w_gate[0], w_up[0], w_down[0]), capacity)

time: 142 us -> 149 us (1.049)
  Pallas kernels: 138 us -> 146 us
    pallas_call x1, Pallas kernels: 138 us -> 146 us  [layer(): pl.pallas_call(layer_kernel, out_shape=jax.ShapeDtypeStruct((tokens, part...]
    dynamic_slice x2 -> x0, local copies, waits for them, and re-layouts: 1.51 us -> none  [the longest x1 0.82 us: plane_body(): lax.dynamic_slice_in_dim(expert_ids, z * share, share, 0)]
    unnamed x4 -> x2, local copies, waits for them, and re-layouts: 2.31 us -> 3.03 us
where the time goes in v3:
time: 149 us
  Pallas kernels  146 us (98%)
  local copies, waits for them, and re-layouts  3.03 us (2%)
    pallas_call x1, Pallas kernels, layer(): pl.pallas_call(layer_kernel, out_shape=jax.ShapeDtypeStruct((tokens, part...  146 us
    unnamed x2, local copies, waits for them, and re-layouts  3.03 us

profile of v3, /device:TPU:16, one launch (start us, length us, event | category | flops | bytes accessed | tf_op | source)
XLA Modules:
  0.0 148.8 jit_solution(10719067494787806163)
XLA Ops:
  0.0 1.4 copy.14.ids
  1.4 145.7 %layer.1 = bf16[128,768]{1,0:T(8,128)(2,1)} custom-call(bf16[128,1024]{1,0:T(8,128)(2,1)} %query.1, bf16[128,1024]{1,0:T(8,128)(2,1)} %key.1, bf16[128,1024]{1,0:T(8,128)(2,1)} %value.1, f32[8,128]{1,0:T(8,128)} %log_decay.1, f32[1,1024]{1,0:T(1,128)} %bitcast.11, bf16[1024,384]{1,0:T(8,128)(2,1)} %weight.1, bf16[128,3072]{1,0:T(8,128)(2,1)} %residual.1, ...), custom_call_target="tpu_custom_call" | custom-call | tf_op jit(solution)/shard_map/layer/pallas_call | solution.py:716
  147.2 1.6 %copy.16 = bf16[128,768]{1,0:T(8,128)(2,1)} copy(bf16[128,768]{1,0:T(8,128)(2,1)} %layer.1) | data formatting | bytes 393216

commit v4 on v2

--- a/solution.py
+++ b/solution.py
@@ -239,8 +239,7 @@
         copy(first + 4, buffer.at[xn], buffer.at[xn], "ctx", sib),
         copy(first + 5, buffer.at[yn, low], buffer.at[yn, low], "ctx", xn),
         copy(first + 6, buffer.at[yn], buffer.at[yn], "ctx", sib),
-        copy(first + 7, buffer.at[dg, top], buffer.at[dg, top], "ctx", sib),
-        copy(first + 8, buffer.at[dg, low], buffer.at[dg, low], "ctx", sib),
+        copy(first + 7, buffer.at[dg], buffer.at[dg], "ctx", sib),
     ]
 
 
@@ -296,11 +295,11 @@
         inside.append(
             jnp.dot(scores.astype(bf16), value[:, cols], preferred_element_type=f32)
         )
-    for got, onward in ((1, (3, 4)), (2, (5, 6)), (3, (7,)), (5, (8,))):
+    for got, onward in ((1, (3, 4)), (2, (5, 6)), (3, ()), (5, (7,))):
         plan[got].wait_recv()
         for step in onward:
             plan[step].start()
-    for step in (0, 4, 6, 7, 8):
+    for step in (0, 4, 6, 7):
         plan[step].wait_recv()
 
     scales = [None] * states.shape[0]
@@ -361,7 +360,8 @@
     greet([("ctx", b) for b in blocks[1:]] + [("head", p) for p in zs])
     copy = sender(send, recv)
     f32, bf16 = jnp.float32, jnp.bfloat16
-    share, model_width = residual.shape
+    model_width = residual.shape[1]
+    share = residual.shape[0] // (len(zs) + 1)
     mine = pl.ds(pl.multiple_of(z * share, share), share)
     width = weight.shape[1]
 
@@ -377,14 +377,17 @@
     def project(i, block):
         product = jnp.dot(block, weight[...], preferred_element_type=f32).astype(bf16)
         for k in range(len(zs) + 1):
-            part[i, k] = product[k * share : (k + 1) * share]
+            part[k, i] = product[k * share : (k + 1) * share]
+        if i % 2 == 0:
+            return
+        two = pl.ds(i - 1, 2)
         z_in.append([])
         for d, peer in enumerate(zs):
             out_copy = copy(
-                TO_Z + 3 * i + d, part.at[i, peer], from_z.at[i, d], "head", peer
+                TO_Z + 3 * (i // 2) + d, part.at[peer, two], from_z.at[d, two], "head", peer
             )
             out_copy.start()
-            z_in[i].append(out_copy)
+            z_in[-1].append(out_copy)
             sent.append(out_copy)
 
     def arrived(*steps):
@@ -406,20 +409,19 @@
     project(4, rows[blocks[4]])
     arrived(6)
     project(5, rows[blocks[5]])
-    arrived(3)
+    arrived(3, 5)
     plan[7].start()
-    arrived(5)
-    plan[8].start()
     project(6, rows[dg])
-    arrived(7, 8)
+    arrived(7)
     project(7, rows[blocks[7]])
 
     col_copies = []
     for i, block in enumerate(blocks):
-        block_sum = part[i, z].astype(f32)
+        block_sum = part[z, i].astype(f32)
         for d in range(3):
-            z_in[i][d].wait_recv()
-            block_sum += from_z[i, d].astype(f32)
+            if i % 2 == 0:
+                z_in[i // 2][d].wait_recv()
+            block_sum += from_z[d, i].astype(f32)
         summed[i] = block_sum.astype(bf16)
         if i:
             col_copies.append(
@@ -435,7 +437,7 @@
     squares = jnp.zeros((share, 1), f32)
     for k in range(model_width // width):
         cols = slice(k * width, (k + 1) * width)
-        whole = (residual[:, cols].astype(f32) + by_cols[k].astype(f32)).astype(bf16)
+        whole = (residual[mine, cols].astype(f32) + by_cols[k].astype(f32)).astype(bf16)
         mixed[k // per, :, (k % per) * width : (k % per + 1) * width] = whole
         row_values = whole.astype(f32)
         squares += jnp.sum(row_values * row_values, axis=1, keepdims=True)
@@ -485,15 +487,14 @@
             send_on(4, xn, rows_of, sib),
             send_on(5, yn, lower, xn),
             send_on(6, yn, rows_of, sib),
-            send_on(7, dg, upper, sib),
-            send_on(8, dg, lower, sib),
+            send_on(7, dg, rows_of, sib),
         ]
         for step in (1, 2, 0):
             steps[step].start()
         return steps
 
     def relay(steps):
-        for got, onward in ((1, (3, 4)), (2, (5, 6)), (3, (7,)), (5, (8,))):
+        for got, onward in ((1, (3, 4)), (2, (5, 6)), (3, ()), (5, (7,))):
             steps[got].wait_recv()
             for step in onward:
                 steps[step].start()
@@ -513,7 +514,7 @@
         base_copies[-1].start()
     relay(runs[3])
     for steps in runs:
-        for step in (0, 4, 6, 7, 8):
+        for step in (0, 4, 6, 7):
             steps[step].wait_recv()
         sent += steps
     for each in base_copies:
@@ -668,7 +669,8 @@
     query, decay, weight, residual = tensors[0], tensors[3], tensors[5], tensors[6]
     tokens, depth = query.shape
     width = weight.shape[1]
-    share, model_width = residual.shape
+    model_width = residual.shape[1]
+    share = tokens // planes
     units = weights[0].shape[1]
     part_width = model_width // planes
     tiles = units // TILE
@@ -681,8 +683,8 @@
         scratch_shapes=[
             pltpu.VMEM((ctx, depth + 16, depth // decay.shape[0]), bf16),
             pltpu.VMEM((ctx, tokens, depth), bf16),
-            pltpu.VMEM((ctx, planes, share, width), bf16),
-            pltpu.VMEM((ctx, planes - 1, share, width), bf16),
+            pltpu.VMEM((planes, ctx, share, width), bf16),
+            pltpu.VMEM((planes - 1, ctx, share, width), bf16),
             pltpu.VMEM((ctx, share, width), bf16),
             pltpu.VMEM((ctx, share, width), bf16),
             pltpu.VMEM((planes, share, part_width), bf16),
@@ -738,7 +740,7 @@
         log_decay,
         attn_gain[None, :],
         out_weight,
-        lax.dynamic_slice_in_dim(residual, z * share, share, 0),
+        residual,
         moe_gain[None, :],
         router.T,
         lax.dynamic_slice_in_dim(expert_ids, z * share, share, 0),

time: 142 us -> 142 us (level)
  no operation moved by 1% of the time
where the time goes in v4:
time: 142 us; the launch traced here: 141 us
  Pallas kernels  138 us (97%)
  local copies, waits for them, and re-layouts  3.06 us (2%)
    pallas_call x1, Pallas kernels, layer(): pl.pallas_call(layer_kernel, out_shape=jax.ShapeDtypeStruct((tokens, part...  138 us
    unnamed x4, local copies, waits for them, and re-layouts  2.99 us

profile of v4, /device:TPU:16, one launch (start us, length us, event | category | flops | bytes accessed | tf_op | source)
XLA Modules:
  0.0 140.7 jit_solution(13675575969788302619)
XLA Ops:
  0.0 0.0 copy-start
  0.0 0.7 copy-done
  0.7 0.1 constant_dynamic-slice_fusion
  0.8 0.7 copy.15.ids
  1.4 137.6 %layer.1 = bf16[128,768]{1,0:T(8,128)(2,1)} custom-call(bf16[128,1024]{1,0:T(8,128)(2,1)} %query.1, bf16[128,1024]{1,0:T(8,128)(2,1)} %key.1, bf16[128,1024]{1,0:T(8,128)(2,1)} %value.1, f32[8,128]{1,0:T(8,128)} %log_decay.1, f32[1,1024]{1,0:T(1,128)} %bitcast.11, bf16[1024,384]{1,0:T(8,128)(2,1)} %weight.1, bf16[128,3072]{1,0:T(8,128)(2,1)} %residual.1, ...), custom_call_target="tpu_custom_call" | custom-call | tf_op jit(solution)/shard_map/layer/pallas_call | solution.py:678
  139.1 1.6 %copy.17 = bf16[128,768]{1,0:T(8,128)(2,1)} copy(bf16[128,768]{1,0:T(8,128)(2,1)} %layer.1) | data formatting | bytes 393216
Async XLA Ops:
  0.0 0.7 copy-start
